TPU v7x, 32 devices: a whole 2x2x4 slice. The times are simulated.
32 devices in a mesh: dp: 8 (over y, x, core), band: 4 (over z).
Axes of the slice: x: 2, y: 2, z: 4, core: 2. Of those that a mesh axis runs over, the one named last changes fastest.
Arguments:
- visible: bfloat16 [13056, 768], P(('dp', 'band')), may hold values from -6 to 6
- clip_long: int32 [32], P(('dp', 'band')), may hold values from 0 to 1, as said below
- patch_order: int32 [32, 2048], P(('dp', 'band')), may hold values from 0 to 2047, as said below
- embed_weight: bfloat16 [768, 512], replicated, may hold values from -0.21875 to 0.21875
- embed_bias: float32 [512], replicated, may hold values from -3 to 3
- mask_token: float32 [512], replicated, may hold values from -4 to 4
- norm1_gain: float32 [512], replicated, may hold values from 0.1 to 1.9
- norm1_bias: float32 [512], replicated, may hold values from -2 to 2
- qkv_weight: bfloat16 [512, 1536], replicated, may hold values from -0.375 to 0.375
- qv_bias: float32 [2, 512], replicated, may hold values from -2 to 2
- proj_weight: bfloat16 [512, 512], replicated, may hold values from -1 to 1
- proj_bias: float32 [512], replicated, may hold values from -2 to 2
- norm2_gain: float32 [512], replicated, may hold values from 0.1 to 1.9
- norm2_bias: float32 [512], replicated, may hold values from -2 to 2
- fc1_weight: bfloat16 [512, 2048], replicated, may hold values from -0.25 to 0.25
- fc1_bias: float32 [2048], replicated, may hold values from -3 to 3
- fc2_weight: bfloat16 [2048, 512], replicated, may hold values from -0.125 to 0.125
- fc2_bias: float32 [512], replicated, may hold values from -2 to 2
- cotangent: bfloat16 [65536, 512], P(('dp', 'band')), may hold values from -6 to 6
Outputs:
- block_out: bfloat16 [65536, 512], P(('dp', 'band'))
- visible_grad: bfloat16 [13056, 768], P(('dp', 'band'))
- embed_weight_grad: float32 [768, 512], replicated
- embed_bias_grad: float32 [512], replicated
- mask_token_grad: float32 [512], replicated
- norm1_gain_grad: float32 [512], replicated
- norm1_bias_grad: float32 [512], replicated
- qkv_weight_grad: float32 [512, 1536], replicated
- qv_bias_grad: float32 [2, 512], replicated
- proj_weight_grad: float32 [512, 512], replicated
- proj_bias_grad: float32 [512], replicated
- norm2_gain_grad: float32 [512], replicated
- norm2_bias_grad: float32 [512], replicated
- fc1_weight_grad: float32 [512, 2048], replicated
- fc1_bias_grad: float32 [2048], replicated
- fc2_weight_grad: float32 [2048, 512], replicated
- fc2_bias_grad: float32 [512], replicated
Inputs may be any that keep to these rules, and one draw needn't show every extreme that they name: `clip_long`: 1 where a device holds one clip of 256 time frames, 0 where it holds two clips of 128 frames. `patch_order`: row d orders device d's patches (index 8 * frame + frequency bin): where clip_long[d] is 1 a permutation of 0 to 2047; else its first 1024 entries permute 0 to 1023 and the rest permute 2048 / 2 to 2047.
All inputs are finite; a program needn't handle non-finite values.
Results may differ from a plain program's by a relative error of at most 0.013.
The roundings to bfloat16 on the way count: a program that leaves them out, or rounds other values in their place, can miss the bound.
Values may be sent and summed in bfloat16 or wider, within the bound.
No kernel may reach another device: no remote copies, remote signals or barrier semaphores. Data moves between devices by JAX's collectives and lax.ppermute only.
A program may use at most 256 MiB of HBM per device.

v0:
```python
import jax
import jax.numpy as jnp
from jax import lax
from jax.sharding import PartitionSpec as P

HEADS = 16
FREQ = 8
WIN = 4


epsilon = 1e-06


def sincos(places, features):
    halfway = features // 2
    omega = 1.0 / 10000.0 ** (jnp.arange(halfway, dtype=jnp.float32) / halfway)
    angles = places.astype(jnp.float32)[:, None] * omega[None, :]
    return jnp.concatenate([jnp.sin(angles), jnp.cos(angles)], axis=1)


def positions(frame_time, column, features):
    return jnp.concatenate(
        [sincos(frame_time, features // 2), sincos(column, features // 2)], axis=1
    )


def row_layout(long_clip, row_count, freq_bins):
    quarter = row_count // 4
    span = row_count // (2 * freq_bins)
    halfspan = span // 2
    rowid = jnp.arange(row_count, dtype=jnp.int32)
    target = rowid // quarter
    inner = rowid % quarter
    column = target // 2 * WIN + inner % WIN
    local = inner // WIN
    halves = target % 2
    short_time = halves * halfspan + local % halfspan
    short_frame = local // halfspan * span + short_time
    long_frame = halves * span + local
    is_long = long_clip == 1
    frame_time = jnp.where(is_long, long_frame, short_time)
    frame_place = jnp.where(is_long, long_frame, short_frame)
    return (frame_place * freq_bins + column, frame_time, column)


def visible_places(long_clip, ordering, vis_short):
    slots = jnp.arange(2 * vis_short, dtype=jnp.int32)
    halfway = ordering.shape[0] // 2
    paired = jnp.where(slots < vis_short, slots, halfway + slots - vis_short)
    chosen = jnp.where(long_clip == 1, slots, paired)
    return jnp.take(ordering, chosen)


def normalize(values):
    center = values - jnp.mean(values, axis=-1, keepdims=True)
    scaling = lax.rsqrt(jnp.mean(center * center, axis=-1, keepdims=True) + epsilon)
    return (center * scaling, scaling)


def normalize_back(grad_rows, unit_rows, scaling, gain):
    gain_grad = jnp.sum(grad_rows * unit_rows, axis=0)
    bias_grad = jnp.sum(grad_rows, axis=0)
    inner = grad_rows * gain
    back_rows = scaling * (
        inner
        - jnp.mean(inner, axis=-1, keepdims=True)
        - unit_rows * jnp.mean(inner * unit_rows, axis=-1, keepdims=True)
    )
    return (back_rows, gain_grad, bias_grad)


def windowed(values, heads):
    return values.reshape(
        values.shape[0] // (WIN * WIN), WIN * WIN, heads, values.shape[1] // heads
    )


def body(
    visible,
    clip_long,
    patch_order,
    embed_weight,
    embed_bias,
    mask_token,
    norm1_gain,
    norm1_bias,
    qkv_weight,
    qv_bias,
    proj_weight,
    proj_bias,
    norm2_gain,
    norm2_bias,
    fc1_weight,
    fc1_bias,
    fc2_weight,
    fc2_bias,
    cotangent,
):
    features = embed_weight.shape[1]
    heads = HEADS
    factor = (features // heads) ** (-0.5)
    long_clip = clip_long[0]
    ordering = patch_order[0]
    own_rows = ordering.shape[0]
    vis_count = visible.shape[0]
    visible_at = visible_places(long_clip, ordering, vis_count // 2)
    embedded = (
        jnp.dot(visible, embed_weight, preferred_element_type=jnp.float32) + embed_bias
    ).astype(jnp.bfloat16)
    places, frame_time, column = row_layout(long_clip, own_rows, FREQ)
    chooser = (places[:, None] == visible_at[None, :]).astype(jnp.bfloat16)
    masked = 1.0 - jnp.sum(chooser, axis=1, dtype=jnp.float32)
    start = (
        jnp.dot(chooser, embedded, preferred_element_type=jnp.float32)
        + masked[:, None] * mask_token
        + positions(frame_time, column, features)
    )
    inputs = lax.all_to_all(
        start.astype(jnp.bfloat16), "band", split_axis=0, concat_axis=0, tiled=True
    ).astype(jnp.float32)
    row_count = inputs.shape[0]
    unit_one, scale_one = normalize(inputs)
    normed_one = (unit_one * norm1_gain + norm1_bias).astype(jnp.bfloat16)
    projected = jnp.dot(normed_one, qkv_weight, preferred_element_type=jnp.float32)
    query_rows = (projected[:, :features] + qv_bias[0]).astype(jnp.bfloat16)
    key_rows = projected[:, features : 2 * features].astype(jnp.bfloat16)
    value_rows = (projected[:, 2 * features :] + qv_bias[1]).astype(jnp.bfloat16)
    query_win = windowed(query_rows, heads)
    key_win = windowed(key_rows, heads)
    value_win = windowed(value_rows, heads)
    scores = (
        jnp.einsum("wqhe,wkhe->whqk", query_win, key_win, preferred_element_type=jnp.float32)
        * factor
    )
    shifted = jnp.exp(scores - jnp.max(scores, axis=-1, keepdims=True))
    attn_probs = shifted / jnp.sum(shifted, axis=-1, keepdims=True)
    probs_low = attn_probs.astype(jnp.bfloat16)
    attended = (
        jnp.einsum("whqk,wkhe->wqhe", probs_low, value_win, preferred_element_type=jnp.float32)
        .reshape(row_count, features)
        .astype(jnp.bfloat16)
    )
    residual = inputs + (
        jnp.dot(attended, proj_weight, preferred_element_type=jnp.float32) + proj_bias
    )
    unit_two, scale_two = normalize(residual)
    normed_two = (unit_two * norm2_gain + norm2_bias).astype(jnp.bfloat16)
    hidden = jnp.dot(normed_two, fc1_weight, preferred_element_type=jnp.float32) + fc1_bias
    cumulative = 0.5 * (1.0 + lax.erf(hidden * 0.7071067811865476))
    activated = (hidden * cumulative).astype(jnp.bfloat16)
    gelu_slope = cumulative + hidden * jnp.exp(-0.5 * hidden * hidden) * 0.3989422804014327
    block_out = (
        residual + (jnp.dot(activated, fc2_weight, preferred_element_type=jnp.float32) + fc2_bias)
    ).astype(jnp.bfloat16)
    out_grad = cotangent.astype(jnp.float32)
    down_grad = jnp.einsum("nf,nd->fd", activated, cotangent, preferred_element_type=jnp.float32)
    downbias_grad = jnp.sum(out_grad, axis=0)
    hidden_grad = (
        jnp.einsum("nd,fd->nf", cotangent, fc2_weight, preferred_element_type=jnp.float32)
        * gelu_slope
    ).astype(jnp.bfloat16)
    up_grad = jnp.einsum("nd,nf->df", normed_two, hidden_grad, preferred_element_type=jnp.float32)
    upbias_grad = jnp.sum(hidden_grad, axis=0, dtype=jnp.float32)
    normed_grad = jnp.einsum(
        "nf,df->nd", hidden_grad, fc1_weight, preferred_element_type=jnp.float32
    )
    back_two, gaintwo_grad, biastwo_grad = normalize_back(
        normed_grad, unit_two, scale_two, norm2_gain
    )
    residual_grad = out_grad + back_two
    branch_grad = residual_grad.astype(jnp.bfloat16)
    proj_grad = jnp.einsum("nd,ne->de", attended, branch_grad, preferred_element_type=jnp.float32)
    projbias_grad = jnp.sum(branch_grad, axis=0, dtype=jnp.float32)
    attended_grad = jnp.einsum(
        "ne,de->nd", branch_grad, proj_weight, preferred_element_type=jnp.float32
    ).astype(jnp.bfloat16)
    attended_win = windowed(attended_grad, heads)
    probs_grad = jnp.einsum(
        "wqhe,wkhe->whqk", attended_win, value_win, preferred_element_type=jnp.float32
    )
    value_grad = jnp.einsum(
        "whqk,wqhe->wkhe", probs_low, attended_win, preferred_element_type=jnp.float32
    )
    score_grad = (
        attn_probs * (probs_grad - jnp.sum(probs_grad * attn_probs, axis=-1, keepdims=True))
    ).astype(jnp.bfloat16)
    query_grad = (
        jnp.einsum("whqk,wkhe->wqhe", score_grad, key_win, preferred_element_type=jnp.float32)
        * factor
    )
    key_grad = (
        jnp.einsum("whqk,wqhe->wkhe", score_grad, query_win, preferred_element_type=jnp.float32)
        * factor
    )
    joined_grad = jnp.concatenate(
        [
            query_grad.reshape(row_count, features),
            key_grad.reshape(row_count, features),
            value_grad.reshape(row_count, features),
        ],
        axis=1,
    ).astype(jnp.bfloat16)
    qkv_grad = jnp.einsum("nd,ne->de", normed_one, joined_grad, preferred_element_type=jnp.float32)
    qvbias_grad = jnp.stack(
        [
            jnp.sum(joined_grad[:, :features], axis=0, dtype=jnp.float32),
            jnp.sum(joined_grad[:, 2 * features :], axis=0, dtype=jnp.float32),
        ]
    )
    normone_grad = jnp.einsum(
        "ne,de->nd", joined_grad, qkv_weight, preferred_element_type=jnp.float32
    )
    back_one, gainone_grad, biasone_grad = normalize_back(
        normone_grad, unit_one, scale_one, norm1_gain
    )
    input_grad = (residual_grad + back_one).astype(jnp.bfloat16)
    returned = lax.all_to_all(input_grad, "band", split_axis=0, concat_axis=0, tiled=True)
    embed_rows_grad = jnp.einsum("rv,rd->vd", chooser, returned, preferred_element_type=jnp.float32)
    mask_grad = jnp.dot(masked.astype(jnp.bfloat16), returned, preferred_element_type=jnp.float32)
    embed_low = embed_rows_grad.astype(jnp.bfloat16)
    embed_grad = jnp.einsum("ve,vd->ed", visible, embed_low, preferred_element_type=jnp.float32)
    embbias_grad = jnp.sum(embed_rows_grad, axis=0)
    visible_grad = jnp.einsum(
        "vd,ed->ve", embed_low, embed_weight, preferred_element_type=jnp.float32
    ).astype(jnp.bfloat16)
    (
        embed_grad,
        embbias_grad,
        mask_grad,
        gainone_grad,
        biasone_grad,
        qkv_grad,
        qvbias_grad,
        proj_grad,
        projbias_grad,
        gaintwo_grad,
        biastwo_grad,
        up_grad,
        upbias_grad,
        down_grad,
        downbias_grad,
    ) = lax.psum(
        (
            embed_grad,
            embbias_grad,
            mask_grad,
            gainone_grad,
            biasone_grad,
            qkv_grad,
            qvbias_grad,
            proj_grad,
            projbias_grad,
            gaintwo_grad,
            biastwo_grad,
            up_grad,
            upbias_grad,
            down_grad,
            downbias_grad,
        ),
        ("dp", "band"),
    )
    return (
        block_out,
        visible_grad,
        embed_grad,
        embbias_grad,
        mask_grad,
        gainone_grad,
        biasone_grad,
        qkv_grad,
        qvbias_grad,
        proj_grad,
        projbias_grad,
        gaintwo_grad,
        biastwo_grad,
        up_grad,
        upbias_grad,
        down_grad,
        downbias_grad,
    )


def solution(mesh):
    in_specs = (
        P(("dp", "band"), None),
        P(("dp", "band")),
        P(("dp", "band"), None),
        P(),
        P(),
        P(),
        P(),
        P(),
        P(),
        P(),
        P(),
        P(),
        P(),
        P(),
        P(),
        P(),
        P(),
        P(),
        P(("dp", "band"), None),
    )
    out_specs = (
        P(("dp", "band"), None),
        P(("dp", "band"), None),
        P(),
        P(),
        P(),
        P(),
        P(),
        P(),
        P(),
        P(),
        P(),
        P(),
        P(),
        P(),
        P(),
        P(),
        P(),
    )
    return jax.shard_map(body, mesh=mesh, in_specs=in_specs, out_specs=out_specs, check_vma=False)
```

profile of v0, /device:TPU:0, one launch (start us, length us, event | category | flops | bytes accessed | tf_op | source)
XLA Modules:
  0.0 737.0 jit_solution(2265177473946544022)
XLA Ops:
  8.1 3.4 gather_fusion
  12.5 9.0 %multiply_sine_fusion.1 = (f32[2048,128]{1,0:T(8,128)S(1)}, f32[2048,128]{1,0:T(8,128)}, f32[2048,128]{1,0:T(8,128)}, f32[2048,128]{1,0:T(8,128)}) fusion(f32[128]{0:T(128)S(1)} %negate_power_fusion, f32[2048]{0:T(1024)S(1)} %get-tuple-element.123, f32[2048]{0:T(1024)S(1)} %fusion.94), kind=kLoop, calls=%fused_computation.92 | loop fusion | flops 524288 | bytes 4211200 | tf_op jit(solution)/shard_map/sin | solution.py:18
  21.5 5.6 fusion.39
  27.2 6.6 all-to-all-start
  33.9 48.3 %all-to-all-done = bf16[4,512,512]{2,1,0:T(8,128)(2,1)} async-done(((bf16[4,512,512]{2,1,0:T(8,128)(2,1)}), bf16[4,512,512]{2,1,0:T(8,128)(2,1)}, u32[]{:S(2)}, u32[]{:S(2)}) %all-to-all-start) | async-done | bytes 2097184 | tf_op jit(solution)/shard_map/all_to_all | solution.py:118
  84.3 2.4 fusion.41
  89.5 3.4 fusion.108
  94.5 3.2 fusion.37
  97.7 10.2 %reshape.324 = bf16[128,16,16,32]{3,2,1,0:T(8,128)(2,1)} reshape(bf16[2048,512]{1,0:T(8,128)(2,1)} %get-tuple-element.93) | data formatting | bytes 4194304 | tf_op jit(solution)/shard_map/reshape | solution.py:73
  107.9 10.2 %reshape.325 = bf16[128,16,16,32]{3,2,1,0:T(8,128)(2,1)} reshape(bf16[2048,512]{1,0:T(8,128)(2,1)} %slice.35) | data formatting | bytes 4194304 | tf_op jit(solution)/shard_map/reshape | solution.py:73
  118.2 10.2 %reshape.323 = bf16[128,16,16,32]{3,2,1,0:T(8,128)(2,1)} reshape(bf16[2048,512]{1,0:T(8,128)(2,1)} %get-tuple-element.94) | data formatting | bytes 4194304 | tf_op jit(solution)/shard_map/reshape | solution.py:73
  128.4 13.8 %fusion.19 = f32[128,16,16,16]{2,3,1,0:T(8,128)} fusion(bf16[128,16,16,32]{3,2,1,0:T(8,128)(2,1)} %reshape.325, bf16[128,16,16,32]{3,2,1,0:T(8,128)(2,1)} %reshape.324), kind=kOutput, calls=%fused_computation.31 | convolution fusion | flops 33554432 | bytes 6291456 | tf_op jit(solution)/shard_map/wqhe,wkhe->whqk/dot_general | solution.py:132
  142.2 20.3 %fusion.105 = (f32[128,16,16]{2,1,0:T(8,128)S(1)}, f32[128,16,16,16]{2,3,1,0:T(8,128)}) fusion(f32[128,16,16,16]{2,3,1,0:T(8,128)} %fusion.19), kind=kOutput, calls=%fused_computation.181 | output fusion | flops 2097167 | bytes 4325376 | tf_op jit(solution)/shard_map/sub | solution.py:135
  162.6 13.9 %convert_bitcast_fusion.1 = bf16[128,16,16,32]{3,1,2,0:T(8,128)(2,1)} fusion(bf16[128,16,16,32]{3,2,1,0:T(8,128)(2,1)} %reshape.323, f32[128,16,16,16]{2,3,1,0:T(8,128)} %get-tuple-element.109, f32[128,16,16]{2,1,0:T(8,128)S(1)} %get-tuple-element.108), kind=kOutput, calls=%fused_computation.20 | convolution fusion | flops 35651584 | bytes 6422528 | tf_op jit(solution)/shard_map/whqk,wkhe->wqhe/dot_general | solution.py:139
  176.4 10.8 %copy.66 = bf16[128,16,16,32]{3,2,1,0:T(8,128)(2,1)} copy(bf16[128,16,16,32]{3,1,2,0:T(8,128)(2,1)} %convert_bitcast_fusion.1) | data formatting | bytes 4194304 | tf_op jit(solution)/shard_map/convert_element_type | solution.py:141
  187.3 12.0 %convert_element_type.124 = bf16[2048,512]{1,0:T(8,128)(2,1)} reshape(bf16[128,16,16,32]{3,2,1,0:T(8,128)(2,1)} %copy.66) | data formatting | bytes 4194304 | tf_op jit(solution)/shard_map/convert_element_type | solution.py:141
  199.3 3.9 fusion.106
  204.2 11.5 %multiply_convert_fusion.3 = (bf16[2048,2048]{1,0:T(8,128)(2,1)}, f32[2048,2048]{1,0:T(8,128)}) fusion(f32[2048]{0:T(1024)S(1)} %copy-done.45, bf16[512,2048]{1,0:T(8,128)(2,1)S(1)} %copy-done, f32[2048,512]{1,0:T(8,128)S(1)} %get-tuple-element.111, f32[512]{0:T(512)S(1)} %copy-done.49, f32[512]{0:T(512)S(1)} %copy-done.38, f32[2048]{0:T(1024)S(1)} %add_rsqrt_fusion, ...), kind=kOutput, calls=%fused_computation.14 | convolution fusion | flops 4325376000 | bytes 31485952 | tf_op jit(solution)/shard_map/dot_general | solution.py:148
  215.7 13.6 %convert_reduce_fusion = (f32[2048]{0:T(1024)}, bf16[2048,2048]{1,0:T(8,128)(2,1)S(1)}) fusion(f32[2048,2048]{1,0:T(8,128)} %get-tuple-element.113, f32[2048]{0:T(1024)S(1)} %copy-done.45, bf16[2048,512]{1,0:T(8,128)(2,1)S(1)} %copy-done.13, bf16[2048,512]{1,0:T(8,128)(2,1)S(1)} %copy-done.42), kind=kOutput, calls=%fused_computation.9 | convolution fusion | flops 4349491200 | bytes 29376512 | tf_op jit(solution)/shard_map/nd,fd->nf/dot_general | solution.py:159
  229.3 6.9 multiply_reduce_fusion.2
  236.2 2.6 convert_reduce_fusion.3
  238.9 2.3 fusion.96
  242.5 7.0 reshape.326
  249.5 13.0 %convert_bitcast_fusion = bf16[128,16,16,32]{3,1,2,0:T(8,128)(2,1)} fusion(bf16[128,16,16,32]{3,2,1,0:T(8,128)(2,1)} %reshape.326, f32[128,16,16,16]{2,3,1,0:T(8,128)} %get-tuple-element.109, f32[128,16,16]{2,1,0:T(8,128)S(1)} %get-tuple-element.108), kind=kOutput, calls=%fused_computation.19 | convolution fusion | flops 35651584 | bytes 6422528 | tf_op jit(solution)/shard_map/whqk,wqhe->wkhe/dot_general | solution.py:181
  262.5 20.6 %multiply_reduce_fusion = (f32[128,16,16]{2,1,0:T(8,128)S(1)}, f32[128,16,16,16]{2,3,1,0:T(8,128)}) fusion(f32[128,16,16,16]{2,3,1,0:T(8,128)} %get-tuple-element.109, f32[128,16,16]{2,1,0:T(8,128)S(1)} %get-tuple-element.108, bf16[128,16,16,32]{3,2,1,0:T(8,128)(2,1)} %reshape.323, bf16[128,16,16,32]{3,2,1,0:T(8,128)(2,1)} %reshape.326), kind=kOutput, calls=%fused_computation.13 | convolution fusion | flops 35094528 | bytes 8650752 | tf_op jit(solution)/shard_map/wqhe,wkhe->whqk/dot_general | solution.py:178
  283.1 14.9 %multiply_convert_fusion.2 = bf16[128,16,16,16]{2,3,1,0:T(8,128)(2,1)} fusion(f32[128,16,16,16]{2,3,1,0:T(8,128)} %get-tuple-element.116, f32[128,16,16]{2,1,0:T(8,128)S(1)} %get-tuple-element.115, f32[128,16,16,16]{2,3,1,0:T(8,128)} %get-tuple-element.109, f32[128,16,16]{2,1,0:T(8,128)S(1)} %get-tuple-element.108), kind=kLoop, calls=%fused_computation.12 | loop fusion | flops 2097152 | bytes 5505024 | tf_op jit(solution)/shard_map/convert_element_type | solution.py:186
  298.0 13.5 %fusion.30 = bf16[128,16,16,32]{3,1,2,0:T(8,128)(2,1)} fusion(bf16[128,16,16,16]{2,3,1,0:T(8,128)(2,1)} %multiply_convert_fusion.2, bf16[128,16,16,32]{3,2,1,0:T(8,128)(2,1)} %reshape.324), kind=kOutput, calls=%fused_computation.36 | convolution fusion | flops 35651584 | bytes 5242880 | tf_op jit(solution)/shard_map/whqk,wqhe->wkhe/dot_general | solution.py:192
  311.5 10.3 %fusion.27 = bf16[128,16,16,32]{3,1,2,0:T(8,128)(2,1)} fusion(bf16[128,16,16,16]{2,3,1,0:T(8,128)(2,1)} %multiply_convert_fusion.2, bf16[128,16,16,32]{3,2,1,0:T(8,128)(2,1)} %reshape.325), kind=kOutput, calls=%fused_computation.35 | convolution fusion | flops 35651584 | bytes 5242880 | tf_op jit(solution)/shard_map/whqk,wkhe->wqhe/dot_general | solution.py:188
  321.8 10.8 %copy.75 = bf16[128,16,16,32]{3,2,1,0:T(8,128)(2,1)} copy(bf16[128,16,16,32]{3,1,2,0:T(8,128)(2,1)} %convert_bitcast_fusion) | data formatting | bytes 4194304 | tf_op jit(solution)/shard_map/whqk,wqhe->wkhe/transpose | solution.py:181
  332.7 10.9 %reshape.329 = bf16[2048,512]{1,0:T(8,128)(2,1)S(1)} reshape(bf16[128,16,16,32]{3,2,1,0:T(8,128)(2,1)} %copy.75) | data formatting | bytes 4194304 | tf_op jit(solution)/shard_map/reshape | solution.py:199
  343.6 10.8 %copy.71 = bf16[128,16,16,32]{3,2,1,0:T(8,128)(2,1)} copy(bf16[128,16,16,32]{3,1,2,0:T(8,128)(2,1)} %fusion.27) | data formatting | bytes 4194304 | tf_op jit(solution)/shard_map/mul | solution.py:188
  354.4 12.1 %reshape.327 = bf16[2048,512]{1,0:T(8,128)(2,1)} reshape(bf16[128,16,16,32]{3,2,1,0:T(8,128)(2,1)} %copy.71) | data formatting | bytes 4194304 | tf_op jit(solution)/shard_map/reshape | solution.py:197
  366.6 10.8 %copy.73 = bf16[128,16,16,32]{3,2,1,0:T(8,128)(2,1)} copy(bf16[128,16,16,32]{3,1,2,0:T(8,128)(2,1)} %fusion.30) | data formatting | bytes 4194304 | tf_op jit(solution)/shard_map/mul | solution.py:192
  377.4 12.0 %reshape.328 = bf16[2048,512]{1,0:T(8,128)(2,1)} reshape(bf16[128,16,16,32]{3,2,1,0:T(8,128)(2,1)} %copy.73) | data formatting | bytes 4194304 | tf_op jit(solution)/shard_map/reshape | solution.py:198
  393.2 5.2 fusion.110
  398.5 6.0 fusion.54
  404.6 3.8 fusion.53
  408.3 4.5 all-to-all-start.1
  413.1 10.6 %fusion.111 = f32[2048,512]{1,0:T(8,128)} fusion(bf16[2048,2048]{1,0:T(8,128)(2,1)} %get-tuple-element.112, bf16[2048,512]{1,0:T(8,128)(2,1)} %param.37), kind=kOutput, calls=%fused_computation.187 | convolution fusion | flops 4294967296 | bytes 14680064 | tf_op jit(solution)/shard_map/nf,nd->fd/dot_general | solution.py:156
  423.8 10.3 %fusion.102 = f32[512,2048]{1,0:T(8,128)} fusion(bf16[2048,2048]{1,0:T(8,128)(2,1)} %copy-done.52, f32[2048,512]{1,0:T(8,128)S(1)} %copy-done.5, f32[512]{0:T(512)S(1)} %copy-done.50, f32[512]{0:T(512)S(1)} %copy-done.39, f32[2048]{0:T(1024)S(1)} %copy-done.25, f32[2048]{0:T(1024)S(1)} %copy-done.19), kind=kOutput, calls=%fused_computation.178 | convolution fusion | flops 4300210176 | bytes 16797696 | tf_op jit(solution)/shard_map/nd,nf->df/dot_general | solution.py:162
  434.1 26.4 %all-to-all-done.1 = bf16[4,512,512]{2,1,0:T(8,128)(2,1)} async-done(((bf16[4,512,512]{2,1,0:T(8,128)(2,1)}), bf16[4,512,512]{2,1,0:T(8,128)(2,1)}, u32[]{:S(2)}, u32[]{:S(2)}) %all-to-all-start.1) | async-done | bytes 2097184 | tf_op jit(solution)/shard_map/all_to_all | solution.py:217
  460.5 2.7 fusion.107
  466.0 2.2 convert_reduce_fusion.5
  468.3 11.3 %add_convert_fusion = bf16[2048,512]{1,0:T(8,128)(2,1)} fusion(f32[2048,512]{1,0:T(8,128)S(1)} %copy-done.6, bf16[2048,2048]{1,0:T(8,128)(2,1)} %get-tuple-element.112, bf16[2048,512]{1,0:T(8,128)(2,1)} %param.35, f32[512]{0:T(512)S(1)} %copy-done.51), kind=kOutput, calls=%fused_computation.75 | convolution fusion | flops 4298113024 | bytes 16779264 | tf_op jit(solution)/shard_map/dot_general | solution.py:153
  481.6 40.1 %all-reduce = (f32[512]{0:T(512)}, f32[512]{0:T(512)}, f32[512]{0:T(512)}, f32[512]{0:T(512)}, f32[2,512]{1,0:T(2,128)}, /*index=5*/f32[512]{0:T(512)}, f32[512]...) all-reduce(f32[512]{0:T(512)S(1)} %get-tuple-element.118, ...), channel_id=1, replica_groups=mesh['dp'=8,'band'=4] {'dp','band'}, use_global_device_ids=true, to_apply=%region_14.15 | all-reduce | flops 7168 | bytes 57344 | tf_op jit(solution)/shard_map/psum | solution.py:242
  523.1 193.0 %all-reduce.4.cloned.1.call-done = (f32[768,512]{0,1:T(8,128)}, f32[512,1536]{1,0:T(8,128)}, f32[512,512]{1,0:T(8,128)}, f32[512,2048]{1,0:T(8,128)}, f32[2048,512]{1,0:T(8,128)}) async-done(((f32[768,512]{0,1:T(8,128)}, f32[512,1536]{1,0:T(8,128)}, f32[512,512]{1,0:T(8,128)}, f32[512,2048]{1,0:T(8,128)}, f32[2048,512]{1,0:T(8,128)}), (f32[768,512]{0,1:T(8,128)}, f32[512,1536]{1,0:T(8,128)}, ...) | async-done | bytes 14155792 | tf_op jit(solution)/shard_map/psum | solution.py:242
  716.1 3.1 copy.76
  719.2 3.9 copy.117
  (144 shorter events, 26.7 us)
Async XLA Ops:
  7.2 196.9 %copy-start = (bf16[512,2048]{1,0:T(8,128)(2,1)S(1)}, bf16[512,2048]{1,0:T(8,128)(2,1)}, u32[]{:S(2)}) copy-start(bf16[512,2048]{1,0:T(8,128)(2,1)} %param.33) | copy-start | bytes 6291460
  7.2 14.3 %copy-start.46 = (f32[512]{0:T(512)S(1)}, f32[512]{0:T(512)}, u32[]{:S(2)}) copy-start(f32[512]{0:T(512)} %param.24) | copy-start | bytes 6148
  7.2 14.3 %copy-start.47 = (f32[512]{0:T(512)S(1)}, f32[512]{0:T(512)}, u32[]{:S(2)}) copy-start(f32[512]{0:T(512)} %param.23) | copy-start | bytes 6148
  8.1 19.1 %copy-start.26 = (s32[2048]{0:T(1024)}, s32[2048]{0:T(1024)S(1)}, u32[]{:S(2)}) copy-start(s32[2048]{0:T(1024)S(1)} %get-tuple-element.122) | copy-start | bytes 24580
  11.5 15.7 %copy-start.32 = (s32[408]{0:T(512)}, s32[408]{0:T(512)S(1)}, u32[]{:S(2)}) copy-start(s32[408]{0:T(512)S(1)} %and_select_fusion) | copy-start | bytes 4900
  27.2 6.7 copy-start.36
  27.2 60.1 %copy-start.34 = (f32[512]{0:T(512)S(1)}, f32[512]{0:T(512)}, u32[]{:S(2)}) copy-start(f32[512]{0:T(512)} %param.25) | copy-start | bytes 6148
  27.2 60.1 %copy-start.37 = (f32[512]{0:T(512)S(1)}, f32[512]{0:T(512)}, u32[]{:S(2)}) copy-start(f32[512]{0:T(512)} %param.26) | copy-start | bytes 6148
  27.2 54.9 %all-to-all-start = ((bf16[4,512,512]{2,1,0:T(8,128)(2,1)}), bf16[4,512,512]{2,1,0:T(8,128)(2,1)}, u32[]{:S(2)}, u32[]{:S(2)}) async-start(bf16[4,512,512]{2,1,0:T(8,128)(2,1)} %bitcast.97), calls=%async_computation | async-start | bytes 4194304 | tf_op jit(solution)/shard_map/all_to_all | solution.py:118
  82.1 7.3 copy-start.43
  84.2 2.5 copy-start.20
  89.5 3.4 copy-start.11
  187.3 12.0 %copy-start.48 = (f32[512]{0:T(512)S(1)}, f32[512]{0:T(512)}, u32[]{:S(2)}) copy-start(f32[512]{0:T(512)} %param.30) | copy-start | bytes 6148
  203.2 33.0 %copy-start.4 = (f32[2048,512]{1,0:T(8,128)}, f32[2048,512]{1,0:T(8,128)S(1)}, u32[]{:S(2)}) copy-start(f32[2048,512]{1,0:T(8,128)S(1)} %get-tuple-element.111) | copy-start | bytes 12582916
  203.2 33.0 %copy-start.18 = (f32[2048]{0:T(1024)}, f32[2048]{0:T(1024)S(1)}, u32[]{:S(2)}) copy-start(f32[2048]{0:T(1024)S(1)} %broadcast_multiply_fusion.4) | copy-start | bytes 24580
  204.1 32.1 %copy-start.24 = (f32[2048]{0:T(1024)}, f32[2048]{0:T(1024)S(1)}, u32[]{:S(2)}) copy-start(f32[2048]{0:T(1024)S(1)} %add_rsqrt_fusion) | copy-start | bytes 24580
  204.2 11.6 %copy-start.13 = (bf16[2048,512]{1,0:T(8,128)(2,1)S(1)}, bf16[2048,512]{1,0:T(8,128)(2,1)}, u32[]{:S(2)}) copy-start(bf16[2048,512]{1,0:T(8,128)(2,1)} %param.37) | copy-start | bytes 6291460
  204.2 11.6 %copy-start.42 = (bf16[2048,512]{1,0:T(8,128)(2,1)S(1)}, bf16[2048,512]{1,0:T(8,128)(2,1)}, u32[]{:S(2)}) copy-start(bf16[2048,512]{1,0:T(8,128)(2,1)} %param.35) | copy-start | bytes 6291460
  229.3 6.9 copy-start.52
  236.2 2.7 copy-start.7
  238.9 2.4 copy-start.17
  393.2 5.2 copy-start.21
  393.2 5.2 copy-start.23
  393.2 5.2 copy-start.35
  393.2 5.2 copy-start.44
  398.5 6.1 copy-start.3
  408.3 52.2 %all-to-all-start.1 = ((bf16[4,512,512]{2,1,0:T(8,128)(2,1)}), bf16[4,512,512]{2,1,0:T(8,128)(2,1)}, u32[]{:S(2)}, u32[]{:S(2)}) async-start(bf16[4,512,512]{2,1,0:T(8,128)(2,1)} %bitcast.96), calls=%async_computation.1 | async-start | bytes 4194304 | tf_op jit(solution)/shard_map/all_to_all | solution.py:217
  412.8 303.3 %all-reduce.4.cloned.1.call-start = ((), (), s32[]{:S(2)}) async-start(), calls=%async_computation.2 | async-start | bytes 28311552 | tf_op jit(solution)/shard_map/psum | solution.py:242
  413.0 10.7 %copy-start.5 = (f32[2048,512]{1,0:T(8,128)S(1)}, f32[2048,512]{1,0:T(8,128)}, u32[]{:S(2)}) copy-start(f32[2048,512]{1,0:T(8,128)} %copy-done.4) | copy-start | bytes 12582916
  413.1 10.7 %copy-start.19 = (f32[2048]{0:T(1024)S(1)}, f32[2048]{0:T(1024)}, u32[]{:S(2)}) copy-start(f32[2048]{0:T(1024)} %copy-done.18) | copy-start | bytes 24580
  413.1 10.7 %copy-start.25 = (f32[2048]{0:T(1024)S(1)}, f32[2048]{0:T(1024)}, u32[]{:S(2)}) copy-start(f32[2048]{0:T(1024)} %copy-done.24) | copy-start | bytes 24580
  413.1 10.7 %copy-start.39 = (f32[512]{0:T(512)S(1)}, f32[512]{0:T(512)}, u32[]{:S(2)}) copy-start(f32[512]{0:T(512)} %param.31) | copy-start | bytes 6148
  413.1 10.7 %copy-start.50 = (f32[512]{0:T(512)S(1)}, f32[512]{0:T(512)}, u32[]{:S(2)}) copy-start(f32[512]{0:T(512)} %param.32) | copy-start | bytes 6148
  423.8 36.7 %copy-start.27 = (s32[2048]{0:T(1024)S(1)}, s32[2048]{0:T(1024)}, u32[]{:S(2)}) copy-start(s32[2048]{0:T(1024)} %copy-done.26) | copy-start | bytes 24580
  423.8 36.7 %copy-start.33 = (s32[408]{0:T(512)S(1)}, s32[408]{0:T(512)}, u32[]{:S(2)}) copy-start(s32[408]{0:T(512)} %copy-done.32) | copy-start | bytes 4900
  434.1 29.1 %copy-start.16 = (bf16[408,768]{1,0:T(8,128)(2,1)S(1)}, bf16[408,768]{1,0:T(8,128)(2,1)}, u32[]{:S(2)}) copy-start(bf16[408,768]{1,0:T(8,128)(2,1)} %param.19) | copy-start | bytes 1880068
  465.0 3.2 copy-start.6
  465.0 3.2 copy-start.51
  468.2 13.4 %copy-start.29 = (f32[512]{0:T(512)S(1)}, f32[512]{0:T(512)}, u32[]{:S(2)}) copy-start(f32[512]{0:T(512)} %get-tuple-element.91) | copy-start | bytes 6148
  468.2 13.4 %copy-start.30 = (f32[512]{0:T(512)S(1)}, f32[512]{0:T(512)}, u32[]{:S(2)}) copy-start(f32[512]{0:T(512)} %get-tuple-element.95) | copy-start | bytes 6148
  468.2 13.4 %copy-start.31 = (f32[2048]{0:T(1024)S(1)}, f32[2048]{0:T(1024)}, u32[]{:S(2)}) copy-start(f32[2048]{0:T(1024)} %get-tuple-element.120) | copy-start | bytes 24580
  468.2 13.4 %copy-start.40 = (f32[512]{0:T(512)S(1)}, f32[512]{0:T(512)}, u32[]{:S(2)}) copy-start(f32[512]{0:T(512)} %get-tuple-element.68) | copy-start | bytes 6148
  468.3 13.4 %copy-start.41 = (f32[512]{0:T(512)S(1)}, f32[512]{0:T(512)}, u32[]{:S(2)}) copy-start(f32[512]{0:T(512)} %get-tuple-element.74) | copy-start | bytes 6148
  468.3 53.5 %copy-start.15 = (bf16[768,512]{1,0:T(8,128)(2,1)S(1)}, bf16[768,512]{1,0:T(8,128)(2,1)}, u32[]{:S(2)}) copy-start(bf16[768,512]{1,0:T(8,128)(2,1)} %param.22) | copy-start | bytes 2359300
  716.1 7.0 copy-start.14
  719.2 4.9 copy-start.10
  724.1 3.7 copy-start.9
  724.1 5.7 copy-start.1
  (8 other events, 10.2 us)
Sparse Core Ops, SparseCore 0:
  465.1 250.9 all-reduce.3
where the time goes:
time: 743 us; the launch traced here: 737 us
  waiting for transfers between devices  268 us (36%)
  matrix products  185 us (25%)
  local copies, waits for them, and re-layouts  152 us (20%)
  other arithmetic  65 us (9%)
  blocking collectives  40.1 us (5%)
  between operations  15.8 us (2%)
  starting transfers between devices  11.3 us (2%)
    psum x1, waiting for transfers between devices, body(): lax.psum((embed_grad, embbias_grad, mask_grad, gainone_grad, biasone_grad...  193 us
    all_to_all x1, waiting for transfers between devices, body(): lax.all_to_all(start.astype(jnp.bfloat16), 'band', split_axis=0, concat_a...  48.3 us
    psum x1, blocking collectives, body(): lax.psum((embed_grad, embbias_grad, mask_grad, gainone_grad, biasone_grad...  40.1 us
    reshape x4, local copies, waits for them, and re-layouts, windowed(): values.reshape(values.shape[0] // (WIN * WIN), WIN * WIN, heads, values.s...  37.7 us
    all_to_all x1, waiting for transfers between devices, body(): lax.all_to_all(input_grad, 'band', split_axis=0, concat_axis=0, tiled=True)  26.4 us
    convert_element_type x2, local copies, waits for them, and re-layouts, body(): attended = jnp.einsum('whqk,wkhe->wqhe', probs_low, value_win, preferred_...  22.8 us
    dot_general x1, matrix products, body(): jnp.einsum('wqhe,wkhe->whqk', attended_win, value_win, preferred_element_...  20.6 us
    sub x1, other arithmetic, body(): shifted = jnp.exp(scores - jnp.max(scores, axis=-1, keepdims=True))  20.3 us
  transfers between devices with their start and end apart: 3, of which 3 were waited for; matrix products, arithmetic and copies ran while one was open for 5% of the time, Pallas kernels for 0%

commit v1 on v0

v1 whole, which is shorter than its diff:
```python
import functools

import jax
import jax.numpy as jnp
from jax import lax
from jax.experimental import pallas as pl
from jax.experimental.pallas import tpu as pltpu
from jax.sharding import PartitionSpec as P

HEADS = 16
FREQ = 8
WIN = 4
EPS = 1e-06
BF = jnp.bfloat16
F32 = jnp.float32
LANES = 128
MIB = 1024 * 1024


def row_layout(is_long, rowid, row_count):
    quarter = row_count // 4
    span = row_count // (2 * FREQ)
    halfspan = span // 2
    target = rowid // quarter
    inner = rowid % quarter
    column = target // 2 * WIN + inner % WIN
    local = inner // WIN
    halves = target % 2
    if is_long:
        frame_time = halves * span + local
        frame = frame_time
    else:
        frame_time = halves * halfspan + local % halfspan
        frame = local // halfspan * span + frame_time
    return frame * FREQ + column, frame_time, column


def sincos_rows(places, features):
    halfway = features // 2
    omega = 1.0 / 10000.0 ** (jnp.arange(halfway, dtype=F32) / halfway)
    angles = omega[:, None] * places.astype(F32)[None, :]
    return jnp.concatenate([jnp.sin(angles), jnp.cos(angles)], axis=0)


def positions_t(frame_time, column, features):
    return jnp.concatenate(
        [sincos_rows(frame_time, features // 2), sincos_rows(column, features // 2)], axis=0
    )


def mm(a, b):
    return lax.dot_general(a, b, (((1,), (0,)), ((), ())), preferred_element_type=F32)


def mm_nt(a, b):
    return lax.dot_general(a, b, (((1,), (1,)), ((), ())), preferred_element_type=F32)


def lane_block(t):
    return pl.ds(pl.multiple_of(t * LANES, LANES), LANES)


def window_of_lane(rows, columns):
    lane = lax.broadcasted_iota(jnp.int32, (rows, columns), 1)
    return (lane % LANES) // (WIN * WIN)


def compact(square, win):
    size = WIN * WIN
    out = square[0:size]
    for w in range(1, LANES // size):
        out = jnp.where(win == w, square[w * size : (w + 1) * size], out)
    return out


def expand(rows, win):
    size = WIN * WIN
    return jnp.concatenate(
        [jnp.where(win == w, rows, 0.0).astype(BF) for w in range(LANES // size)], axis=0
    )


def stacked(wide):
    return jnp.concatenate(
        [wide[:, j * LANES : (j + 1) * LANES] for j in range(wide.shape[1] // LANES)], axis=0
    )


def heads_apart(group, width):
    count = LANES // width
    blocks = []
    for j in range(count):
        parts = []
        if j:
            parts.append(jnp.zeros((j * width, LANES), BF))
        parts.append(group[j * width : (j + 1) * width])
        if j < count - 1:
            parts.append(jnp.zeros(((count - 1 - j) * width, LANES), BF))
        blocks.append(jnp.concatenate(parts, axis=0))
    return jnp.concatenate(blocks, axis=1)


def heads_of(wide, width):
    return jnp.concatenate(
        [
            wide[j * width : (j + 1) * width, j * LANES : (j + 1) * LANES]
            for j in range(LANES // width)
        ],
        axis=0,
    )


def normalize_t(x):
    count = x.shape[0]
    center = x - jnp.sum(x, axis=0, keepdims=True) * (1.0 / count)
    var = jnp.sum(center * center, axis=0, keepdims=True) * (1.0 / count)
    scale = lax.rsqrt(var + EPS)
    return center * scale, scale


def normalize_back_t(grad, unit, scale, gain):
    count = grad.shape[0]
    inner = grad * gain
    mean = jnp.sum(inner, axis=0, keepdims=True) * (1.0 / count)
    mixed = jnp.sum(inner * unit, axis=0, keepdims=True) * (1.0 / count)
    return scale * (inner - mean - unit * mixed)


def lane_sums(acc):
    return jnp.sum(acc.T, axis=0, keepdims=True)


def chooser_t(vis, place):
    return jnp.where(vis == place, 1.0, 0.0)


C_MASK, C_G1, C_B1, C_QB, C_VB, C_PB, C_G2, C_B2, C_F2B = range(9)


def forward_kernel(
    sk, flags,
    emb, vis, place, pos_long, pos_short, cols, fc1b, cot,
    wqkv_t, wproj_t, w1_t, w1, w2_t, w2,
    block_out, x_t, qkv_t, probs, o_t, act_t, gh_t, c_out, gx1_t, sums,
    emb_pad, a_t, x1_t, c_t, cot_t, unit2, scale2, wide, acc,
):
    features = x_t.shape[0]
    rows = x_t.shape[1]
    tiles = rows // LANES
    width = features // HEADS
    factor = width ** (-0.5)
    step = pl.program_id(0)
    is_long = flags[step] == 1

    def col(i):
        return cols[:, i : i + 1]

    count = emb.shape[0]
    emb_pad[0:count, :] = emb[...]
    emb_pad[count:, :] = jnp.zeros((emb_pad.shape[0] - count, features), BF)
    wide[...] = mm(emb_pad[...].T, chooser_t(vis[...], place[...]).astype(BF))

    def entry_step(t, _):
        sl = lane_block(t)
        filled = jnp.sum(chooser_t(vis[...], place[:, sl]), axis=0, keepdims=True)
        pos = jnp.where(is_long, pos_long[:, sl], pos_short[:, sl])
        start = (wide[:, sl] + (1.0 - filled) * col(C_MASK)) + pos
        start = start.astype(BF)
        x_t[:, sl] = start
        unit, _scale = normalize_t(start.astype(F32))
        a_t[:, sl] = (unit * col(C_G1) + col(C_B1)).astype(BF)
        cot_t[:, sl] = cot[pl.ds(pl.multiple_of(t * LANES, LANES), LANES), :].T
        return 0

    lax.fori_loop(0, tiles, entry_step, 0)

    for i, bias in ((0, C_QB), (1, None), (2, C_VB)):
        part = pl.ds(i * features, features)
        prod = mm(wqkv_t[part, :], a_t[...])
        if bias is not None:
            prod = prod + col(bias)
        qkv_t[part, :] = prod.astype(BF)

    def attention_step(t, _):
        sl = lane_block(t)
        win = window_of_lane(WIN * WIN, 4 * LANES)
        for g in range(features // LANES):
            q_g = qkv_t[pl.ds(g * LANES, LANES), sl]
            k_g = qkv_t[pl.ds(features + g * LANES, LANES), sl]
            v_g = qkv_t[pl.ds(2 * features + g * LANES, LANES), sl]
            scores = compact(mm(k_g.T, heads_apart(q_g, width)), win) * factor
            shifted = jnp.exp(scores - jnp.max(scores, axis=0, keepdims=True))
            prob = shifted / jnp.sum(shifted, axis=0, keepdims=True)
            probs[t, :, g * 4 * LANES : (g + 1) * 4 * LANES] = prob
            mixed = mm(v_g, expand(prob, win))
            o_t[pl.ds(g * LANES, LANES), sl] = heads_of(mixed, width).astype(BF)
        return 0

    lax.fori_loop(0, tiles, attention_step, 0)

    wide[...] = mm(wproj_t[...], o_t[...])

    def norm2_step(t, _):
        sl = lane_block(t)
        x1 = x_t[:, sl].astype(F32) + (wide[:, sl] + col(C_PB))
        x1_t[:, sl] = x1
        unit, scale = normalize_t(x1)
        unit2[:, sl] = unit
        scale2[:, sl] = scale
        low = (unit * col(C_G2) + col(C_B2)).astype(BF)
        c_t[:, sl] = low
        c_out[pl.ds(pl.multiple_of(t * LANES, LANES), LANES), :] = low.T
        return 0

    lax.fori_loop(0, tiles, norm2_step, 0)

    chunk = features

    def hidden_step(f, _):
        part = pl.ds(pl.multiple_of(f * chunk, chunk), chunk)
        hidden = mm(w1_t[part, :], c_t[...]) + fc1b[part, :]
        cumulative = 0.5 * (1.0 + lax.erf(hidden * 0.7071067811865476))
        act_t[part, :] = (hidden * cumulative).astype(BF)
        slope = cumulative + hidden * jnp.exp(-0.5 * hidden * hidden) * 0.3989422804014327
        gact = mm(w2[part, :], cot_t[...])
        gh_t[part, :] = (gact * slope).astype(BF)
        return 0

    lax.fori_loop(0, w1_t.shape[0] // chunk, hidden_step, 0)

    half = features // 2

    def out_step(i, _):
        part = pl.ds(pl.multiple_of(i * half, half), half)
        wide[part, :] = mm(w2_t[part, :], act_t[...])
        return 0

    lax.fori_loop(0, 2, out_step, 0)

    def finish_step(t, _):
        sl = lane_block(t)
        out = x1_t[:, sl] + (wide[:, sl] + col(C_F2B))
        block_out[pl.ds(pl.multiple_of(t * LANES, LANES), LANES), :] = out.astype(BF).T
        return 0

    lax.fori_loop(0, tiles, finish_step, 0)

    def back_step(i, _):
        part = pl.ds(pl.multiple_of(i * half, half), half)
        wide[part, :] = mm(w1[part, :], gh_t[...])
        return 0

    lax.fori_loop(0, 2, back_step, 0)

    acc[...] = jnp.zeros_like(acc)

    def norm2_back_step(t, _):
        sl = lane_block(t)
        gc = wide[:, sl]
        unit = unit2[:, sl]
        acc[0] += gc * unit
        acc[1] += gc
        back = normalize_back_t(gc, unit, scale2[:, sl], col(C_G2))
        gx1_t[:, sl] = cot_t[:, sl].astype(F32) + back
        return 0

    lax.fori_loop(0, tiles, norm2_back_step, 0)
    sums[...] = jnp.zeros_like(sums)
    sums[0:1, :] = lane_sums(acc[0])
    sums[1:2, :] = lane_sums(acc[1])


def backward_kernel(
    sk,
    vis, place, cols, x_t, qkv_t, probs, gx1_t, wproj, wqkv,
    gqkv_t, a_out, gy_out, gemb, sums,
    gy_t, go_t, gx, wide, acc,
):
    features = x_t.shape[0]
    rows = x_t.shape[1]
    tiles = rows // LANES
    width = features // HEADS
    factor = width ** (-0.5)

    def col(i):
        return cols[:, i : i + 1]

    acc[...] = jnp.zeros_like(acc)

    def branch_step(t, _):
        sl = lane_block(t)
        low = gx1_t[:, sl].astype(BF)
        gy_t[:, sl] = low
        gy_out[pl.ds(pl.multiple_of(t * LANES, LANES), LANES), :] = low.T
        acc[0] += low.astype(F32)
        return 0

    lax.fori_loop(0, tiles, branch_step, 0)
    go_t[...] = mm(wproj[...], gy_t[...]).astype(BF)

    def attention_step(t, _):
        sl = lane_block(t)
        win = window_of_lane(WIN * WIN, 4 * LANES)
        for g in range(features // LANES):
            part = pl.ds(g * LANES, LANES)
            q_g = qkv_t[part, sl]
            k_g = qkv_t[pl.ds(features + g * LANES, LANES), sl]
            v_g = qkv_t[pl.ds(2 * features + g * LANES, LANES), sl]
            go_g = go_t[part, sl]
            gp = compact(mm(v_g.T, heads_apart(go_g, width)), win)
            prob = probs[t, :, g * 4 * LANES : (g + 1) * 4 * LANES]
            gs = prob * (gp - jnp.sum(gp * prob, axis=0, keepdims=True))
            gs_wide = expand(gs, win)
            prob_wide = expand(prob, win)
            gq = (heads_of(mm(k_g, gs_wide), width) * factor).astype(BF)
            gk = (heads_of(mm_nt(q_g, stacked(gs_wide)), width) * factor).astype(BF)
            gv = heads_of(mm_nt(go_g, stacked(prob_wide)), width).astype(BF)
            gqkv_t[part, sl] = gq
            gqkv_t[pl.ds(features + g * LANES, LANES), sl] = gk
            gqkv_t[pl.ds(2 * features + g * LANES, LANES), sl] = gv
            acc[1, part] += gq.astype(F32)
            acc[2, part] += gv.astype(F32)
        return 0

    lax.fori_loop(0, tiles, attention_step, 0)

    half = features // 2

    def back_step(i, _):
        part = pl.ds(pl.multiple_of(i * half, half), half)
        wide[part, :] = mm(wqkv[part, :], gqkv_t[...])
        return 0

    lax.fori_loop(0, 2, back_step, 0)

    def norm1_back_step(t, _):
        sl = lane_block(t)
        rows_t = pl.ds(pl.multiple_of(t * LANES, LANES), LANES)
        unit, scale = normalize_t(x_t[:, sl].astype(F32))
        a_out[rows_t, :] = (unit * col(C_G1) + col(C_B1)).astype(BF).T
        ga = wide[:, sl]
        acc[3] += ga * unit
        acc[4] += ga
        back = normalize_back_t(ga, unit, scale, col(C_G1))
        low = (gx1_t[:, sl] + back).astype(BF)
        gx[rows_t, :] = low.T
        filled = jnp.sum(chooser_t(vis[...], place[:, sl]), axis=0, keepdims=True)
        acc[5] += low.astype(F32) * (1.0 - filled)
        return 0

    lax.fori_loop(0, tiles, norm1_back_step, 0)
    chosen = mm(chooser_t(vis[...], place[...]).astype(BF), gx[...])
    gemb[...] = chosen[0 : gemb.shape[0]].astype(BF)
    sums[...] = jnp.zeros_like(sums)
    for i in range(6):
        sums[i : i + 1, :] = lane_sums(acc[i])


def product_kernel(left, right, out):
    out[...] = mm(left[...], right[...]).astype(BF)


def product_bias_kernel(left, right, out, bias):
    out[...] = mm(left[...], right[...]).astype(BF)
    total = left[:, 0:LANES].astype(F32)
    for i in range(1, left.shape[1] // LANES):
        total += left[:, i * LANES : (i + 1) * LANES].astype(F32)
    bias[...] = jnp.sum(total.T, axis=0, keepdims=True)


def product(left, right, with_bias=False, block=256):
    m, depth = left.shape
    n = right.shape[1]
    steps = m // block
    out_shape = [jax.ShapeDtypeStruct((m, n), BF)]
    out_specs = [pl.BlockSpec((block, n), lambda i: (i, 0))]
    if with_bias:
        out_shape.append(jax.ShapeDtypeStruct((steps, 1, block), F32))
        out_specs.append(pl.BlockSpec((None, 1, block), lambda i: (i, 0, 0)))
    out = pl.pallas_call(
        product_bias_kernel if with_bias else product_kernel,
        grid=(steps,),
        in_specs=[
            pl.BlockSpec((block, depth), lambda i: (i, 0)),
            pl.BlockSpec((depth, n), lambda i: (0, 0)),
        ],
        out_specs=out_specs,
        out_shape=out_shape,
        cost_estimate=pl.CostEstimate(
            flops=2 * m * n * depth, bytes_accessed=2 * (m * depth + n * depth + m * n),
            transcendentals=0,
        ),
        compiler_params=pltpu.CompilerParams(vmem_limit_bytes=32 * MIB),
    )(left, right)
    return out if with_bias else out[0]


def whole(shape):
    zeros = (0,) * len(shape)
    return pl.BlockSpec(shape, lambda i, *_: zeros, pipeline_mode=pl.Buffered(1))


def forward(sk, flags, emb, vis, place, pos_long, pos_short, cols, fc1b, cot, weights):
    count, features = emb.shape[1:]
    rows = place.shape[2]
    total = cot.shape[0]
    hidden = fc1b.shape[0]
    n = emb.shape[0]
    tiles = rows // LANES
    per_k = lambda k, *_: (k, 0, 0)
    lanes_s = lambda k, sk, *_: (0, sk[k])
    rows_s = lambda k, sk, *_: (sk[k], 0)
    s = jax.ShapeDtypeStruct
    return pl.pallas_call(
        forward_kernel,
        grid_spec=pltpu.PrefetchScalarGridSpec(
            num_scalar_prefetch=2,
            grid=(n,),
            in_specs=[
                pl.BlockSpec((None, count, features), per_k),
                pl.BlockSpec((None, rows, 1), per_k),
                pl.BlockSpec((None, 1, rows), per_k),
                whole(pos_long.shape),
                whole(pos_short.shape),
                whole(cols.shape),
                whole(fc1b.shape),
                pl.BlockSpec((rows, features), rows_s),
            ]
            + [whole(w.shape) for w in weights],
            out_specs=[
                pl.BlockSpec((rows, features), rows_s),
                pl.BlockSpec((features, rows), lanes_s),
                pl.BlockSpec((3 * features, rows), lanes_s),
                pl.BlockSpec((None, tiles, WIN * WIN, HEADS * LANES), lambda k, sk, *_: (sk[k], 0, 0, 0)),
                pl.BlockSpec((features, rows), lanes_s),
                pl.BlockSpec((hidden, rows), lanes_s),
                pl.BlockSpec((hidden, rows), lanes_s),
                pl.BlockSpec((rows, features), rows_s),
                pl.BlockSpec((features, rows), lanes_s),
                pl.BlockSpec((None, 8, features), per_k),
            ],
            scratch_shapes=[
                pltpu.VMEM((rows, features), BF),
                pltpu.VMEM((features, rows), BF),
                pltpu.VMEM((features, rows), F32),
                pltpu.VMEM((features, rows), BF),
                pltpu.VMEM((features, rows), BF),
                pltpu.VMEM((features, rows), F32),
                pltpu.VMEM((1, rows), F32),
                pltpu.VMEM((features, rows), F32),
                pltpu.VMEM((2, features, LANES), F32),
            ],
        ),
        out_shape=[
            s((total, features), BF),
            s((features, total), BF),
            s((3 * features, total), BF),
            s((total // rows, tiles, WIN * WIN, HEADS * LANES), F32),
            s((features, total), BF),
            s((hidden, total), BF),
            s((hidden, total), BF),
            s((total, features), BF),
            s((features, total), F32),
            s((n, 8, features), F32),
        ],
        cost_estimate=pl.CostEstimate(
            flops=2 * n * rows * features * (4 * features + 4 * hidden + 2 * rows),
            bytes_accessed=28 * MIB,
            transcendentals=3 * n * rows * hidden,
        ),
        compiler_params=pltpu.CompilerParams(vmem_limit_bytes=56 * MIB),
    )(sk, flags, emb, vis, place, pos_long, pos_short, cols, fc1b, cot, *weights)


def backward(sk, count, vis, place, cols, x_t, qkv_t, probs, gx1_t, wproj, wqkv):
    features, total = x_t.shape
    n, _, rows = place.shape
    tiles = rows // LANES
    per_k = lambda k, *_: (k, 0, 0)
    lanes_s = lambda k, sk, *_: (0, sk[k])
    rows_s = lambda k, sk, *_: (sk[k], 0)
    s = jax.ShapeDtypeStruct
    return pl.pallas_call(
        backward_kernel,
        grid_spec=pltpu.PrefetchScalarGridSpec(
            num_scalar_prefetch=1,
            grid=(n,),
            in_specs=[
                pl.BlockSpec((None, rows, 1), per_k),
                pl.BlockSpec((None, 1, rows), per_k),
                whole(cols.shape),
                pl.BlockSpec((features, rows), lanes_s),
                pl.BlockSpec((3 * features, rows), lanes_s),
                pl.BlockSpec((None, tiles, WIN * WIN, HEADS * LANES), lambda k, sk, *_: (sk[k], 0, 0, 0)),
                pl.BlockSpec((features, rows), lanes_s),
                whole(wproj.shape),
                whole(wqkv.shape),
            ],
            out_specs=[
                pl.BlockSpec((3 * features, rows), lanes_s),
                pl.BlockSpec((rows, features), rows_s),
                pl.BlockSpec((rows, features), rows_s),
                pl.BlockSpec((None, count, features), per_k),
                pl.BlockSpec((None, 8, features), per_k),
            ],
            scratch_shapes=[
                pltpu.VMEM((features, rows), BF),
                pltpu.VMEM((features, rows), BF),
                pltpu.VMEM((rows, features), BF),
                pltpu.VMEM((features, rows), F32),
                pltpu.VMEM((6, features, LANES), F32),
            ],
        ),
        out_shape=[
            s((3 * features, total), BF),
            s((total, features), BF),
            s((total, features), BF),
            s((n, count, features), BF),
            s((n, 8, features), F32),
        ],
        cost_estimate=pl.CostEstimate(
            flops=2 * n * rows * features * (4 * features + 5 * rows),
            bytes_accessed=22 * MIB,
            transcendentals=0,
        ),
        compiler_params=pltpu.CompilerParams(vmem_limit_bytes=56 * MIB),
    )(sk, vis, place, cols, x_t, qkv_t, probs, gx1_t, wproj, wqkv)


def shift(x, by, size):
    return lax.ppermute(x, "band", [(i, (i + by) % size) for i in range(size)])


def swap(x, bit, size):
    return lax.ppermute(x, "dp", [(i, i ^ (1 << bit)) for i in range(size)])


def pick(x, index):
    return lax.dynamic_index_in_dim(x, index, 0, keepdims=False)


def reduce_rows(grad, bits, dp, band):
    me, z = lax.axis_index("dp"), lax.axis_index("band")
    for bit in bits:
        mine = (me >> bit) & 1
        halves = grad.reshape(2, grad.shape[0] // 2, grad.shape[1])
        got = swap(pick(halves, 1 - mine), bit, dp)
        grad = (pick(halves, mine).astype(F32) + got.astype(F32)).astype(BF)
    parts = grad.reshape(band, grad.shape[0] // band, grad.shape[1])
    total = pick(parts, z).astype(F32)
    for d in range(1, band):
        total = total + shift(pick(parts, (z + d) % band), d, band).astype(F32)
    return total.astype(BF)


def gather_rows(share, bits, dp, band):
    me, z = lax.axis_index("dp"), lax.axis_index("band")
    full = jnp.zeros((band,) + share.shape, share.dtype)
    full = lax.dynamic_update_index_in_dim(full, share, z, 0)
    for d in range(1, band):
        full = lax.dynamic_update_index_in_dim(full, shift(share, d, band), (z - d) % band, 0)
    full = full.reshape(band * share.shape[0], share.shape[1])
    for bit in reversed(bits):
        mine = (me >> bit) & 1
        got = swap(full, bit, dp)
        full = jnp.where(
            mine == 0, jnp.concatenate([full, got], 0), jnp.concatenate([got, full], 0)
        )
    return full


def reduce_small(x, bits, dp, band):
    for bit in bits:
        x = x + swap(x, bit, dp)
    total = x
    step = 1
    while step < band:
        total = total + lax.ppermute(total, "band", [(i, i ^ step) for i in range(band)])
        step *= 2
    return total


def body(
    dp, band,
    visible, clip_long, patch_order, embed_weight, embed_bias, mask_token,
    norm1_gain, norm1_bias, qkv_weight, qv_bias, proj_weight, proj_bias,
    norm2_gain, norm2_bias, fc1_weight, fc1_bias, fc2_weight, fc2_bias, cotangent,
):
    features = embed_weight.shape[1]
    hidden = fc1_weight.shape[1]
    total = patch_order.shape[1]
    rows = total // band
    vis_count = visible.shape[0]
    count = -(-vis_count // 16) * 16
    z = lax.axis_index("band")
    bits = []
    while (1 << len(bits)) < dp:
        bits.append(len(bits))

    order = patch_order[0]
    half = vis_count // 2
    middle = total // 2
    visible_at = jnp.where(
        clip_long[0] == 1,
        order[:vis_count],
        jnp.concatenate([order[:half], order[middle : middle + vis_count - half]]),
    )
    note = jnp.concatenate(
        [visible_at, jnp.full((rows - vis_count - 1,), -1, jnp.int32), clip_long]
    ).reshape(1, rows)
    notes = jnp.concatenate([note] + [shift(note, d, band) for d in range(1, band)], axis=0)
    flags = notes[:, rows - 1]
    vis = jnp.where(jnp.arange(rows)[None, :] < vis_count, notes, -1)[:, :, None]
    sk = (z - jnp.arange(band, dtype=jnp.int32)) % band

    embedded = (
        jnp.dot(visible, embed_weight, preferred_element_type=F32) + embed_bias
    ).astype(BF)
    embedded = jnp.pad(embedded, ((0, count - vis_count), (0, 0)))
    ring = [embedded]
    for _ in range(1, band):
        ring.append(shift(ring[-1], 1, band))
    emb = jnp.stack(ring)

    rowid = z * rows + jnp.arange(rows, dtype=jnp.int32)
    place_long, time_long, column = row_layout(True, rowid, total)
    place_short, time_short, _ = row_layout(False, rowid, total)
    place = jnp.where(flags[:, None] == 1, place_long[None, :], place_short[None, :])[:, None, :]
    pos_long = positions_t(time_long, column, features)
    pos_short = positions_t(time_short, column, features)

    cols = jnp.stack(
        [
            mask_token, norm1_gain, norm1_bias, qv_bias[0], qv_bias[1], proj_bias,
            norm2_gain, norm2_bias, fc2_bias,
        ]
        + [jnp.zeros_like(fc2_bias)] * 7,
        axis=1,
    )
    weights = (qkv_weight.T, proj_weight.T, fc1_weight.T, fc1_weight, fc2_weight.T, fc2_weight)
    block_out, x_t, qkv_t, probs, o_t, act_t, gh_t, c, gx1_t, sums_f = forward(
        sk, flags, emb, vis, place, pos_long, pos_short, cols, fc1_bias[:, None], cotangent, weights
    )

    fc2_grad = product(act_t, cotangent)
    fc1_grad_t, fc1b_grad = product(gh_t, c, with_bias=True)
    gqkv_t, a, gy, gemb, sums_b = backward(
        sk, count, vis, place, cols, x_t, qkv_t, probs, gx1_t, proj_weight, qkv_weight
    )
    qkv_grad_t = product(gqkv_t, a)
    proj_grad = product(o_t, gy)

    back = gemb[1]
    for k in list(range(2, band)) + [0]:
        back = shift(back, 1, band) + gemb[k]
    back = back[:vis_count]
    embed_grad = jnp.einsum("ve,vd->ed", visible, back, preferred_element_type=F32).astype(BF)
    visible_grad = jnp.einsum(
        "vd,ed->ve", back, embed_weight, preferred_element_type=F32
    ).astype(BF)

    sums_f = jnp.sum(sums_f, axis=0)
    sums_b = jnp.sum(sums_b, axis=0)
    small = jnp.concatenate(
        [
            sums_f[0:2],
            sums_b[0:6],
            jnp.sum(cotangent, axis=0, dtype=F32)[None],
            jnp.sum(back, axis=0, dtype=F32)[None],
            fc1b_grad.reshape(hidden // features, features),
        ],
        axis=0,
    )
    small = reduce_small(small, bits, dp, band)

    outs = []
    for grad in (fc2_grad, fc1_grad_t, qkv_grad_t, proj_grad, embed_grad):
        share = reduce_rows(grad, bits, dp, band)
        outs.append(gather_rows(share, bits, dp, band))
    fc2_grad, fc1_grad_t, qkv_grad_t, proj_grad, embed_grad = outs

    return (
        block_out,
        visible_grad,
        embed_grad.astype(F32),
        small[9],
        small[7],
        small[5],
        small[6],
        qkv_grad_t.T.astype(F32),
        jnp.stack([small[3], small[4]]),
        proj_grad.astype(F32),
        small[2],
        small[0],
        small[1],
        fc1_grad_t.T.astype(F32),
        small[10:].reshape(hidden),
        fc2_grad.astype(F32),
        small[8],
    )


def solution(mesh):
    split = P(("dp", "band"), None)
    in_specs = (split, P(("dp", "band")), split) + (P(),) * 15 + (split,)
    out_specs = (split, split) + (P(),) * 15
    return jax.shard_map(
        functools.partial(body, mesh.shape["dp"], mesh.shape["band"]),
        mesh=mesh,
        in_specs=in_specs,
        out_specs=out_specs,
        check_vma=False,
    )
```

time: 743 us -> 423 us (0.57)
  matrix products: 185 us -> 4.42 us
  waiting for transfers between devices: 268 us -> 106 us
  Pallas kernels: 0 us -> 150 us
  local copies, waits for them, and re-layouts: 152 us -> 44 us
  starting transfers between devices: 11.3 us -> 74.1 us
  blocking collectives: 40.1 us -> 0 us
  other arithmetic: 65 us -> 40.3 us
  between operations: 15.8 us -> 2.5 us
    psum x1 -> x0, waiting for transfers between devices: 193 us -> none  [body(): lax.psum((embed_grad, embbias_grad, mask_grad, gainone_grad, biasone_grad...]
    dot_general x23 -> x3, matrix products: 185 us -> 4.42 us  [the longest x1 1.56 us: body(): jnp.dot(visible, embed_weight, preferred_element_type=F32) + embed_bias]
    pallas_call x0 -> x6, Pallas kernels: none -> 150 us  [the longest x1 83.5 us: forward(): pl.pallas_call(forward_kernel, grid_spec=pltpu.PrefetchScalarGridSpec(num...]
    ppermute x0 -> x74, waiting for transfers between devices: none -> 106 us  [the longest x39 71.6 us: shift(): return lax.ppermute(x, 'band', [(i, (i + by) % size) for i in range(size)])]
    all_to_all x2 -> x0, waiting for transfers between devices: 74.7 us -> none  [the longest x1 48.3 us: body(): lax.all_to_all(start.astype(jnp.bfloat16), 'band', split_axis=0, concat_a...]
    ppermute x0 -> x74, starting transfers between devices: none -> 74.1 us  [the longest x39 40.9 us: shift(): return lax.ppermute(x, 'band', [(i, (i + by) % size) for i in range(size)])]
    reshape x7 -> x2, local copies, waits for them, and re-layouts: 72.7 us -> 1.51 us  [the longest x1 1.5 us: reduce_rows(): halves = grad.reshape(2, grad.shape[0] // 2, grad.shape[1])]
    psum x1 -> x0, blocking collectives: 40.1 us -> none  [body(): lax.psum((embed_grad, embbias_grad, mask_grad, gainone_grad, biasone_grad...]
  transfers between devices with their start and end apart: 3 -> 74, of which waited for: 3 -> 37; matrix products, arithmetic and copies ran while one was open for 5% -> 17% of each run, Pallas kernels for 0% -> 4%
where the time goes in v1:
time: 423 us; the launch traced here: 422 us
  Pallas kernels  150 us (35%)
  waiting for transfers between devices  106 us (25%)
  starting transfers between devices  74.1 us (18%)
  local copies, waits for them, and re-layouts  44 us (10%)
  other arithmetic  40.3 us (10%)
  matrix products  4.42 us (1%)
    pallas_call x1, Pallas kernels, forward(): pl.pallas_call(forward_kernel, grid_spec=pltpu.PrefetchScalarGridSpec(num...  83.5 us
    ppermute x39, waiting for transfers between devices, shift(): return lax.ppermute(x, 'band', [(i, (i + by) % size) for i in range(size)])  71.6 us
    pallas_call x1, Pallas kernels, backward(): pl.pallas_call(backward_kernel, grid_spec=pltpu.PrefetchScalarGridSpec(nu...  49.8 us
    ppermute x39, starting transfers between devices, shift(): return lax.ppermute(x, 'band', [(i, (i + by) % size) for i in range(size)])  40.9 us
    ppermute x33, waiting for transfers between devices, swap(): return lax.ppermute(x, 'dp', [(i, i ^ 1 << bit) for i in range(size)])  32.6 us
    ppermute x33, starting transfers between devices, swap(): return lax.ppermute(x, 'dp', [(i, i ^ 1 << bit) for i in range(size)])  30.7 us
    unnamed x92, local copies, waits for them, and re-layouts  27.3 us
    pallas_call x4, Pallas kernels, product(): pl.pallas_call(product_bias_kernel if with_bias else product_kernel, grid...  17.1 us
  transfers between devices with their start and end apart: 74, of which 37 were waited for; matrix products, arithmetic and copies ran while one was open for 17% of the time, Pallas kernels for 4%

profile of v1, /device:TPU:0, one launch (start us, length us, event | category | flops | bytes accessed | tf_op | source)
XLA Modules:
  0.0 421.7 jit_solution(9653568154770589568)
XLA Ops:
  2.9 3.0 collective-permute-start
  6.0 2.6 collective-permute-start.1
  13.0 3.8 multiply_sine_fusion
  17.9 3.0 pad_maximum_fusion.1
  21.2 3.9 collective-permute-done.3
  26.7 4.1 copy.109
  30.7 2.4 copy.110
  33.1 2.6 copy.107
  41.5 10.0 %collective-permute-done.5 = bf16[416,512]{1,0:T(8,128)(2,1)S(1)} collective-permute-done((bf16[416,512]{1,0:T(8,128)(2,1)}, bf16[416,512]{1,0:T(8,128)(2,1)S(1)}, u32[]{:S(2)}, u32[]{:S(2)}) %collective-permute-start.5) | collective-permute-done | bytes 426016 | tf_op jit(solution)/shard_map/ppermute | solution.py:531
  51.5 2.6 pad_maximum_fusion.emb
  54.1 83.5 %shard_map.314 = (bf16[2048,512]{1,0:T(8,128)(2,1)}, bf16[512,2048]{1,0:T(8,128)(2,1)}, bf16[1536,2048]{1,0:T(8,128)(2,1)}, f32[4,4,16,2048]{3,2,1,0:T(8,128)}, ...) custom-call(s32[4]{0:T(128)} %and_select_fusion.sk, ...), custom_call_target="tpu_custom_call" | custom-call | flops 23622320128 | bytes 29360128 | tf_op jit(solution)/shard_map/pallas_call | solution.py:414
  137.6 49.8 %shard_map.315 = (bf16[1536,2048]{1,0:T(8,128)(2,1)}, bf16[2048,512]{1,0:T(8,128)(2,1)}, bf16[2048,512]{1,0:T(8,128)(2,1)}, bf16[4,416,512]{2,1,0:T(8,128)(2,1)}, f32[4,8,512]{2,1,0:T(8,128)}) custom-call(s32[4]{0:T(128)} %and_select_fusion.sk, s32[4,512,1]{2,1,0:T(8,128)} %add_select_fusion.vis, s32[4,1,512]{2,1,0:T(1,128)} %broadcast_select_fusion.place, ...), custom_call_target="tpu_custom_call" | custom-call | flops 9663676416 | bytes 23068672 | tf_op jit(solution)/shard_map/pallas_call | solution.py:483
  190.7 3.5 copy-done.9
  194.2 5.7 %shard_map.319 = bf16[2048,512]{1,0:T(8,128)(2,1)S(1)} custom-call(bf16[2048,2048]{1,0:T(8,128)(2,1)S(1)} %copy-done.9, bf16[2048,512]{1,0:T(8,128)(2,1)S(1)} %copy-done.2), custom_call_target="tpu_custom_call" | custom-call | flops 4294967296 | bytes 12582912 | tf_op jit(solution)/shard_map/pallas_call | solution.py:380
  203.0 4.3 %shard_map.317 = bf16[1536,512]{1,0:T(8,128)(2,1)S(1)} custom-call(bf16[1536,2048]{1,0:T(8,128)(2,1)S(1)} %bitcast.263, bf16[2048,512]{1,0:T(8,128)(2,1)S(1)} %copy-done.10), custom_call_target="tpu_custom_call" | custom-call | flops 3221225472 | bytes 9961472 | tf_op jit(solution)/shard_map/pallas_call | solution.py:380
  211.8 2.3 collective-permute-start.42
  217.9 2.1 collective-permute-start.44
  220.0 5.7 %shard_map.316 = (bf16[2048,512]{1,0:T(8,128)(2,1)S(1)}, f32[8,1,256]{2,1,0:T(1,128)S(1)}) custom-call(bf16[2048,2048]{1,0:T(8,128)(2,1)S(1)} %bitcast.265, bf16[2048,512]{1,0:T(8,128)(2,1)S(1)} %copy-done.11), custom_call_target="tpu_custom_call" | custom-call | flops 4294967296 | bytes 12582912 | tf_op jit(solution)/shard_map/pallas_call | solution.py:380
  225.8 2.1 collective-permute-start.45
  230.5 2.7 collective-permute-done.46
  238.5 7.8 %collective-permute-start.48 = (bf16[128,512]{1,0:T(8,128)(2,1)S(1)}, bf16[128,512]{1,0:T(8,128)(2,1)S(1)}, u32[]{:S(2)}, u32[]{:S(2)}) collective-permute-start(bf16[128,512]{1,0:T(8,128)(2,1)S(1)} %maximum_select_fusion.14), channel_id=1, source_target_pairs={{0,8},{4,12},{8,0},{12,4},{16,24},{20,28},{24,16},{28,20},{1,9},{5... | collective-permute-start | bytes 393224 | tf_op jit(solution)/shard_map/ppermute | solution.py:535
  253.3 7.4 %collective-permute-done.7 = bf16[416,512]{1,0:T(8,128)(2,1)S(1)} collective-permute-done((bf16[416,512]{1,0:T(8,128)(2,1)S(1)}, bf16[416,512]{1,0:T(8,128)(2,1)S(1)}, u32[]{:S(2)}, u32[]{:S(2)}) %collective-permute-start.7) | collective-permute-done | bytes 426016 | tf_op jit(solution)/shard_map/ppermute | solution.py:531
  267.7 6.5 %collective-permute-done.8 = bf16[416,512]{1,0:T(8,128)(2,1)S(1)} collective-permute-done((bf16[416,512]{1,0:T(8,128)(2,1)S(1)}, bf16[416,512]{1,0:T(8,128)(2,1)S(1)}, u32[]{:S(2)}, u32[]{:S(2)}) %collective-permute-start.8) | collective-permute-done | bytes 426016 | tf_op jit(solution)/shard_map/ppermute | solution.py:531
  280.5 2.5 collective-permute-done.22
  285.7 2.7 collective-permute-start.31
  299.2 5.0 %collective-permute-done.33 = bf16[48,512]{1,0:T(8,128)(2,1)S(1)} collective-permute-done((bf16[48,512]{1,0:T(8,128)(2,1)S(1)}, bf16[48,512]{1,0:T(8,128)(2,1)S(1)}, u32[]{:S(2)}, u32[]{:S(2)}) %collective-permute-start.33) | collective-permute-done | bytes 49184 | tf_op jit(solution)/shard_map/ppermute | solution.py:531
  305.4 2.9 collective-permute-done.34
  308.3 2.0 collective-permute-start.35
  311.8 2.0 collective-permute-start.52
  315.5 5.6 %collective-permute-done.64 = bf16[256,512]{1,0:T(8,128)(2,1)S(1)} collective-permute-done((bf16[256,512]{1,0:T(8,128)(2,1)S(1)}, bf16[256,512]{1,0:T(8,128)(2,1)S(1)}, u32[]{:S(2)}, u32[]{:S(2)}) %collective-permute-start.64) | collective-permute-done | bytes 262176 | tf_op jit(solution)/shard_map/ppermute | solution.py:535
  321.3 2.6 collective-permute-done.52
  324.6 2.1 collective-permute-start.67
  327.4 3.6 collective-permute-done.66
  331.1 3.0 collective-permute-start.55
  335.2 3.8 collective-permute-done.54
  339.2 3.4 collective-permute-start.69
  343.2 2.2 collective-permute-done.68
  347.9 2.2 collective-permute-start.12
  359.1 3.6 collective-permute-done.15
  362.7 4.7 %collective-permute-done.16 = bf16[24,512]{1,0:T(8,128)(2,1)S(1)} collective-permute-done((bf16[24,512]{1,0:T(8,128)(2,1)S(1)}, bf16[24,512]{1,0:T(8,128)(2,1)S(1)}, u32[]{:S(2)}, u32[]{:S(2)}) %collective-permute-start.16) | collective-permute-done | bytes 24608 | tf_op jit(solution)/shard_map/ppermute | solution.py:531
  368.8 2.4 collective-permute-done.17
  381.4 2.8 collective-permute-done.36
  386.5 11.0 %collective-permute-done.60 = bf16[512,512]{1,0:T(8,128)(2,1)S(1)} collective-permute-done((bf16[512,512]{1,0:T(8,128)(2,1)S(1)}, bf16[512,512]{1,0:T(8,128)(2,1)S(1)}, u32[]{:S(2)}, u32[]{:S(2)}) %collective-permute-start.60) | collective-permute-done | bytes 524320 | tf_op jit(solution)/shard_map/ppermute | solution.py:535
  402.3 2.1 convert_bitcast_fusion.1
  404.4 3.5 copy.116
  408.0 4.2 convert_bitcast_fusion
  412.2 5.3 %copy.117 = f32[512,2048]{1,0:T(8,128)} copy(f32[512,2048]{0,1:T(8,128)} %convert_bitcast_fusion) | data formatting | bytes 8388608
  417.5 4.2 fusion
  (327 shorter events, 108.2 us)
Async XLA Ops:
  2.9 35.2 %collective-permute-start = (s32[1,512]{1,0:T(1,128)S(1)}, s32[1,512]{1,0:T(1,128)S(1)}, u32[]{:S(2)}, u32[]{:S(2)}) collective-permute-start(s32[1,512]{1,0:T(1,128)S(1)} %bitcast.314), channel_id=1, source_target_pairs={{0,1},{1,2},{2,3},{3,0},{4,5},{5,6},{6,7},{7,4},{8,9},{9,10},{10,1... | collective-permute-start | bytes 6152 | tf_op jit(solution)/shard_map/ppermute | solution.py:531
  6.0 32.2 %collective-permute-start.1 = (s32[1,512]{1,0:T(1,128)S(1)}, s32[1,512]{1,0:T(1,128)S(1)}, u32[]{:S(2)}, u32[]{:S(2)}) collective-permute-start(s32[1,512]{1,0:T(1,128)S(1)} %bitcast.315), channel_id=1, source_target_pairs={{0,2},{1,3},{2,0},{3,1},{4,6},{5,7},{6,4},{7,5},{8,10},{9,11},{10,... | collective-permute-start | bytes 6152 | tf_op jit(solution)/shard_map/ppermute | solution.py:531
  8.6 29.6 %collective-permute-start.2 = (s32[1,512]{1,0:T(1,128)S(1)}, s32[1,512]{1,0:T(1,128)S(1)}, u32[]{:S(2)}, u32[]{:S(2)}) collective-permute-start(s32[1,512]{1,0:T(1,128)S(1)} %bitcast.316), channel_id=1, source_target_pairs={{0,3},{1,0},{2,1},{3,2},{4,7},{5,4},{6,5},{7,6},{8,11},{9,8},{10,9... | collective-permute-start | bytes 6152 | tf_op jit(solution)/shard_map/ppermute | solution.py:531
  12.3 12.8 %collective-permute-start.3 = (bf16[416,512]{1,0:T(8,128)(2,1)}, bf16[416,512]{1,0:T(8,128)(2,1)}, u32[]{:S(2)}, u32[]{:S(2)}) collective-permute-start(bf16[416,512]{1,0:T(8,128)(2,1)} %get-tuple-element.153), channel_id=1, source_target_pairs={{0,1},{1,2},{2,3},{3,0},{4,5},{5,6},{6,7},{7,4},{8,9},{9,10},{10,1... | collective-permute-start | bytes 1277960 | tf_op jit(solution)/shard_map/ppermute | solution.py:531
  25.1 14.3 %collective-permute-start.4 = (bf16[416,512]{1,0:T(8,128)(2,1)}, bf16[416,512]{1,0:T(8,128)(2,1)}, u32[]{:S(2)}, u32[]{:S(2)}) collective-permute-start(bf16[416,512]{1,0:T(8,128)(2,1)} %collective-permute-done.3), channel_id=1, source_target_pairs={{0,1},{1,2},{2,3},{3,0},{4,5},{5,6},{6,7},{7,4},{8,9},{9,10},{10,1... | collective-permute-start | bytes 1277960 | tf_op jit(solution)/shard_map/ppermute | solution.py:531
  39.5 12.0 %collective-permute-start.5 = (bf16[416,512]{1,0:T(8,128)(2,1)}, bf16[416,512]{1,0:T(8,128)(2,1)S(1)}, u32[]{:S(2)}, u32[]{:S(2)}) collective-permute-start(bf16[416,512]{1,0:T(8,128)(2,1)} %collective-permute-done.4), channel_id=1, source_target_pairs={{0,1},{1,2},{2,3},{3,0},{4,5},{5,6},{6,7},{7,4},{8,9},{9,10},{10,1... | collective-permute-start | bytes 1277960 | tf_op jit(solution)/shard_map/ppermute | solution.py:531
  190.6 10.7 %collective-permute-start.38 = (bf16[256,512]{1,0:T(8,128)(2,1)S(1)}, bf16[256,512]{1,0:T(8,128)(2,1)S(1)}, u32[]{:S(2)}, u32[]{:S(2)}) collective-permute-start(bf16[256,512]{1,0:T(8,128)(2,1)S(1)} %dynamic-slice_bitcast_fusion.9), channel_id=1, source_target_pairs={{0,4},{4,0},{8,12},{12,8},{16,20},{20,16},{24,28},{28,24},{1,5},{5... | collective-permute-start | bytes 786440 | tf_op jit(solution)/shard_map/ppermute | solution.py:535
  200.9 62.2 %collective-permute-start.62 = (bf16[1024,512]{1,0:T(8,128)(2,1)}, bf16[1024,512]{1,0:T(8,128)(2,1)}, u32[]{:S(2)}, u32[]{:S(2)}) collective-permute-start(bf16[1024,512]{1,0:T(8,128)(2,1)} %dynamic-slice_bitcast_fusion), channel_id=1, source_target_pairs={{0,4},{4,0},{8,12},{12,8},{16,20},{20,16},{24,28},{28,24},{1,5},{5... | collective-permute-start | bytes 3145736 | tf_op jit(solution)/shard_map/ppermute | solution.py:535
  209.8 40.3 %collective-permute-start.26 = (bf16[768,512]{1,0:T(8,128)(2,1)}, bf16[768,512]{1,0:T(8,128)(2,1)}, u32[]{:S(2)}, u32[]{:S(2)}) collective-permute-start(bf16[768,512]{1,0:T(8,128)(2,1)} %dynamic-slice_bitcast_fusion.2), channel_id=1, source_target_pairs={{0,4},{4,0},{8,12},{12,8},{16,20},{20,16},{24,28},{28,24},{1,5},{5... | collective-permute-start | bytes 2359304 | tf_op jit(solution)/shard_map/ppermute | solution.py:535
  217.3 29.0 %collective-permute-start.6 = (bf16[416,512]{1,0:T(8,128)(2,1)}, bf16[416,512]{1,0:T(8,128)(2,1)}, u32[]{:S(2)}, u32[]{:S(2)}) collective-permute-start(bf16[416,512]{1,0:T(8,128)(2,1)} %get-tuple-element.148), channel_id=1, source_target_pairs={{0,1},{1,2},{2,3},{3,0},{4,5},{5,6},{6,7},{7,4},{8,9},{9,10},{10,1... | collective-permute-start | bytes 1277960 | tf_op jit(solution)/shard_map/ppermute | solution.py:531
  217.9 11.6 %collective-permute-start.44 = (bf16[16,512]{1,0:T(8,128)(2,1)S(1)}, bf16[16,512]{1,0:T(8,128)(2,1)S(1)}, u32[]{:S(2)}, u32[]{:S(2)}) collective-permute-start(bf16[16,512]{1,0:T(8,128)(2,1)S(1)} %get-tuple-element.141), channel_id=1, source_target_pairs={{0,1},{1,2},{2,3},{3,0},{4,5},{5,6},{6,7},{7,4},{8,9},{9,10},{10,1... | collective-permute-start | bytes 49160 | tf_op jit(solution)/shard_map/ppermute | solution.py:531
  235.8 41.5 %collective-permute-start.50 = (bf16[1024,512]{1,0:T(8,128)(2,1)}, bf16[1024,512]{1,0:T(8,128)(2,1)}, u32[]{:S(2)}, u32[]{:S(2)}) collective-permute-start(bf16[1024,512]{1,0:T(8,128)(2,1)} %dynamic-slice_bitcast_fusion.1), channel_id=1, source_target_pairs={{0,4},{4,0},{8,12},{12,8},{16,20},{20,16},{24,28},{28,24},{1,5},{5... | collective-permute-start | bytes 3145736 | tf_op jit(solution)/shard_map/ppermute | solution.py:535
  238.5 11.4 %collective-permute-start.48 = (bf16[128,512]{1,0:T(8,128)(2,1)S(1)}, bf16[128,512]{1,0:T(8,128)(2,1)S(1)}, u32[]{:S(2)}, u32[]{:S(2)}) collective-permute-start(bf16[128,512]{1,0:T(8,128)(2,1)S(1)} %maximum_select_fusion.14), channel_id=1, source_target_pairs={{0,8},{4,12},{8,0},{12,4},{16,24},{20,28},{24,16},{28,20},{1,9},{5... | collective-permute-start | bytes 393224 | tf_op jit(solution)/shard_map/ppermute | solution.py:535
  247.5 13.3 %collective-permute-start.7 = (bf16[416,512]{1,0:T(8,128)(2,1)S(1)}, bf16[416,512]{1,0:T(8,128)(2,1)S(1)}, u32[]{:S(2)}, u32[]{:S(2)}) collective-permute-start(bf16[416,512]{1,0:T(8,128)(2,1)S(1)} %bitcast_add_fusion.1), channel_id=1, source_target_pairs={{0,1},{1,2},{2,3},{3,0},{4,5},{5,6},{6,7},{7,4},{8,9},{9,10},{10,1... | collective-permute-start | bytes 1277960 | tf_op jit(solution)/shard_map/ppermute | solution.py:531
  250.0 11.9 %collective-permute-start.49 = (bf16[256,512]{1,0:T(8,128)(2,1)S(1)}, bf16[256,512]{1,0:T(8,128)(2,1)S(1)}, u32[]{:S(2)}, u32[]{:S(2)}) collective-permute-start(bf16[256,512]{1,0:T(8,128)(2,1)S(1)} %maximum_select_fusion.12), channel_id=1, source_target_pairs={{0,4},{4,0},{8,12},{12,8},{16,20},{20,16},{24,28},{28,24},{1,5},{5... | collective-permute-start | bytes 786440 | tf_op jit(solution)/shard_map/ppermute | solution.py:535
  251.5 15.2 %collective-permute-start.27 = (bf16[384,512]{1,0:T(8,128)(2,1)S(1)}, bf16[384,512]{1,0:T(8,128)(2,1)S(1)}, u32[]{:S(2)}, u32[]{:S(2)}) collective-permute-start(bf16[384,512]{1,0:T(8,128)(2,1)S(1)} %dynamic-slice_bitcast_fusion.5), channel_id=1, source_target_pairs={{0,8},{4,12},{8,0},{12,4},{16,24},{20,28},{24,16},{28,20},{1,9},{5... | collective-permute-start | bytes 1179656 | tf_op jit(solution)/shard_map/ppermute | solution.py:535
  261.8 12.4 %collective-permute-start.8 = (bf16[416,512]{1,0:T(8,128)(2,1)S(1)}, bf16[416,512]{1,0:T(8,128)(2,1)S(1)}, u32[]{:S(2)}, u32[]{:S(2)}) collective-permute-start(bf16[416,512]{1,0:T(8,128)(2,1)S(1)} %bitcast_add_fusion), channel_id=1, source_target_pairs={{0,1},{1,2},{2,3},{3,0},{4,5},{5,6},{6,7},{7,4},{8,9},{9,10},{10,1... | collective-permute-start | bytes 1277960 | tf_op jit(solution)/shard_map/ppermute | solution.py:531
  266.4 43.9 %collective-permute-start.63 = (bf16[512,512]{1,0:T(8,128)(2,1)}, bf16[512,512]{1,0:T(8,128)(2,1)}, u32[]{:S(2)}, u32[]{:S(2)}) collective-permute-start(bf16[512,512]{1,0:T(8,128)(2,1)} %dynamic-slice_bitcast_fusion.3), channel_id=1, source_target_pairs={{0,8},{4,12},{8,0},{12,4},{16,24},{20,28},{24,16},{28,20},{1,9},{5... | collective-permute-start | bytes 1572872 | tf_op jit(solution)/shard_map/ppermute | solution.py:535
  267.6 15.3 %collective-permute-start.28 = (bf16[192,512]{1,0:T(8,128)(2,1)S(1)}, bf16[192,512]{1,0:T(8,128)(2,1)}, u32[]{:S(2)}, u32[]{:S(2)}) collective-permute-start(bf16[192,512]{1,0:T(8,128)(2,1)S(1)} %dynamic-slice_bitcast_fusion.10), channel_id=1, source_target_pairs={{0,16},{4,20},{8,24},{12,28},{16,0},{20,4},{24,8},{28,12},{1,17},{... | collective-permute-start | bytes 589832 | tf_op jit(solution)/shard_map/ppermute | solution.py:535
  282.9 8.5 %collective-permute-start.23 = (f32[14,512]{1,0:T(8,128)S(1)}, f32[14,512]{1,0:T(8,128)S(1)}, u32[]{:S(2)}, u32[]{:S(2)}) collective-permute-start(f32[14,512]{1,0:T(8,128)S(1)} %add.554), channel_id=1, source_target_pairs={{0,16},{4,20},{8,24},{12,28},{16,0},{20,4},{24,8},{28,12},{1,17},{... | collective-permute-start | bytes 86024 | tf_op jit(solution)/shard_map/ppermute | solution.py:535
  284.6 7.6 %collective-permute-start.29 = (bf16[48,512]{1,0:T(8,128)(2,1)}, bf16[48,512]{1,0:T(8,128)(2,1)S(1)}, u32[]{:S(2)}, u32[]{:S(2)}) collective-permute-start(bf16[48,512]{1,0:T(8,128)(2,1)} %get-tuple-element.160), channel_id=1, source_target_pairs={{0,1},{1,2},{2,3},{3,0},{4,5},{5,6},{6,7},{7,4},{8,9},{9,10},{10,1... | collective-permute-start | bytes 147464 | tf_op jit(solution)/shard_map/ppermute | solution.py:531
  284.6 8.2 %collective-permute-start.30 = (bf16[48,512]{1,0:T(8,128)(2,1)}, bf16[48,512]{1,0:T(8,128)(2,1)S(1)}, u32[]{:S(2)}, u32[]{:S(2)}) collective-permute-start(bf16[48,512]{1,0:T(8,128)(2,1)} %get-tuple-element.162), channel_id=1, source_target_pairs={{0,2},{1,3},{2,0},{3,1},{4,6},{5,7},{6,4},{7,5},{8,10},{9,11},{10,... | collective-permute-start | bytes 147464 | tf_op jit(solution)/shard_map/ppermute | solution.py:531
  285.7 7.1 %collective-permute-start.31 = (bf16[48,512]{1,0:T(8,128)(2,1)S(1)}, bf16[48,512]{1,0:T(8,128)(2,1)S(1)}, u32[]{:S(2)}, u32[]{:S(2)}) collective-permute-start(bf16[48,512]{1,0:T(8,128)(2,1)S(1)} %get-tuple-element.161), channel_id=1, source_target_pairs={{0,3},{1,0},{2,1},{3,2},{4,7},{5,4},{6,5},{7,6},{8,11},{9,8},{10,9... | collective-permute-start | bytes 147464 | tf_op jit(solution)/shard_map/ppermute | solution.py:531
  291.4 20.2 %collective-permute-start.51 = (bf16[512,512]{1,0:T(8,128)(2,1)}, bf16[512,512]{1,0:T(8,128)(2,1)S(1)}, u32[]{:S(2)}, u32[]{:S(2)}) collective-permute-start(bf16[512,512]{1,0:T(8,128)(2,1)} %dynamic-slice_bitcast_fusion.4), channel_id=1, source_target_pairs={{0,8},{4,12},{8,0},{12,4},{16,24},{20,28},{24,16},{28,20},{1,9},{5... | collective-permute-start | bytes 1572872 | tf_op jit(solution)/shard_map/ppermute | solution.py:535
  294.4 19.5 %collective-permute-start.9 = (bf16[384,512]{1,0:T(8,128)(2,1)S(1)}, bf16[384,512]{1,0:T(8,128)(2,1)S(1)}, u32[]{:S(2)}, u32[]{:S(2)}) collective-permute-start(bf16[384,512]{1,0:T(8,128)(2,1)S(1)} %dynamic-slice_bitcast_fusion.6), channel_id=1, source_target_pairs={{0,4},{4,0},{8,12},{12,8},{16,20},{20,16},{24,28},{28,24},{1,5},{5... | collective-permute-start | bytes 1179656 | tf_op jit(solution)/shard_map/ppermute | solution.py:535
  296.3 85.1 %collective-permute-start.25 = (f32[14,512]{1,0:T(8,128)S(1)}, f32[14,512]{1,0:T(8,128)S(1)}, u32[]{:S(2)}, u32[]{:S(2)}) collective-permute-start(f32[14,512]{1,0:T(8,128)S(1)} %add.556), channel_id=1, source_target_pairs={{0,2},{1,3},{2,0},{3,1},{4,6},{5,7},{6,4},{7,5},{8,10},{9,11},{10,... | collective-permute-start | bytes 86024 | tf_op jit(solution)/shard_map/ppermute | solution.py:578
  308.3 64.4 %collective-permute-start.35 = (bf16[192,512]{1,0:T(8,128)(2,1)S(1)}, bf16[192,512]{1,0:T(8,128)(2,1)S(1)}, u32[]{:S(2)}, u32[]{:S(2)}) collective-permute-start(bf16[192,512]{1,0:T(8,128)(2,1)S(1)} %bitcast.297), channel_id=1, source_target_pairs={{0,16},{4,20},{8,24},{12,28},{16,0},{20,4},{24,8},{28,12},{1,17},{... | collective-permute-start | bytes 589832 | tf_op jit(solution)/shard_map/ppermute | solution.py:535
  311.5 9.6 %collective-permute-start.64 = (bf16[256,512]{1,0:T(8,128)(2,1)S(1)}, bf16[256,512]{1,0:T(8,128)(2,1)S(1)}, u32[]{:S(2)}, u32[]{:S(2)}) collective-permute-start(bf16[256,512]{1,0:T(8,128)(2,1)S(1)} %dynamic-slice_bitcast_fusion.7), channel_id=1, source_target_pairs={{0,16},{4,20},{8,24},{12,28},{16,0},{20,4},{24,8},{28,12},{1,17},{... | collective-permute-start | bytes 786440 | tf_op jit(solution)/shard_map/ppermute | solution.py:535
  311.8 12.1 %collective-permute-start.52 = (bf16[256,512]{1,0:T(8,128)(2,1)S(1)}, bf16[256,512]{1,0:T(8,128)(2,1)S(1)}, u32[]{:S(2)}, u32[]{:S(2)}) collective-permute-start(bf16[256,512]{1,0:T(8,128)(2,1)S(1)} %dynamic-slice_bitcast_fusion.8), channel_id=1, source_target_pairs={{0,16},{4,20},{8,24},{12,28},{16,0},{20,4},{24,8},{28,12},{1,17},{... | collective-permute-start | bytes 786440 | tf_op jit(solution)/shard_map/ppermute | solution.py:535
  314.0 10.6 %collective-permute-start.10 = (bf16[192,512]{1,0:T(8,128)(2,1)S(1)}, bf16[192,512]{1,0:T(8,128)(2,1)S(1)}, u32[]{:S(2)}, u32[]{:S(2)}) collective-permute-start(bf16[192,512]{1,0:T(8,128)(2,1)S(1)} %dynamic-slice_bitcast_fusion.11), channel_id=1, source_target_pairs={{0,8},{4,12},{8,0},{12,4},{16,24},{20,28},{24,16},{28,20},{1,9},{5... | collective-permute-start | bytes 589832 | tf_op jit(solution)/shard_map/ppermute | solution.py:535
  323.9 7.1 %collective-permute-start.66 = (bf16[64,512]{1,0:T(8,128)(2,1)S(1)}, bf16[64,512]{1,0:T(8,128)(2,1)S(1)}, u32[]{:S(2)}, u32[]{:S(2)}) collective-permute-start(bf16[64,512]{1,0:T(8,128)(2,1)S(1)} %get-tuple-element.156), channel_id=1, source_target_pairs={{0,2},{1,3},{2,0},{3,1},{4,6},{5,7},{6,4},{7,5},{8,10},{9,11},{10,... | collective-permute-start | bytes 196616 | tf_op jit(solution)/shard_map/ppermute | solution.py:531
  324.6 6.6 %collective-permute-start.67 = (bf16[64,512]{1,0:T(8,128)(2,1)S(1)}, bf16[64,512]{1,0:T(8,128)(2,1)S(1)}, u32[]{:S(2)}, u32[]{:S(2)}) collective-permute-start(bf16[64,512]{1,0:T(8,128)(2,1)S(1)} %get-tuple-element.155), channel_id=1, source_target_pairs={{0,3},{1,0},{2,1},{3,2},{4,7},{5,4},{6,5},{7,6},{8,11},{9,8},{10,9... | collective-permute-start | bytes 196616 | tf_op jit(solution)/shard_map/ppermute | solution.py:531
  327.3 6.9 %collective-permute-start.53 = (bf16[64,512]{1,0:T(8,128)(2,1)S(1)}, bf16[64,512]{1,0:T(8,128)(2,1)S(1)}, u32[]{:S(2)}, u32[]{:S(2)}) collective-permute-start(bf16[64,512]{1,0:T(8,128)(2,1)S(1)} %get-tuple-element.157), channel_id=1, source_target_pairs={{0,1},{1,2},{2,3},{3,0},{4,5},{5,6},{6,7},{7,4},{8,9},{9,10},{10,1... | collective-permute-start | bytes 196616 | tf_op jit(solution)/shard_map/ppermute | solution.py:531
  331.0 8.0 %collective-permute-start.54 = (bf16[64,512]{1,0:T(8,128)(2,1)S(1)}, bf16[64,512]{1,0:T(8,128)(2,1)S(1)}, u32[]{:S(2)}, u32[]{:S(2)}) collective-permute-start(bf16[64,512]{1,0:T(8,128)(2,1)S(1)} %get-tuple-element.159), channel_id=1, source_target_pairs={{0,2},{1,3},{2,0},{3,1},{4,6},{5,7},{6,4},{7,5},{8,10},{9,11},{10,... | collective-permute-start | bytes 196616 | tf_op jit(solution)/shard_map/ppermute | solution.py:531
  331.1 8.1 %collective-permute-start.55 = (bf16[64,512]{1,0:T(8,128)(2,1)S(1)}, bf16[64,512]{1,0:T(8,128)(2,1)S(1)}, u32[]{:S(2)}, u32[]{:S(2)}) collective-permute-start(bf16[64,512]{1,0:T(8,128)(2,1)S(1)} %get-tuple-element.158), channel_id=1, source_target_pairs={{0,3},{1,0},{2,1},{3,2},{4,7},{5,4},{6,5},{7,6},{8,11},{9,8},{10,9... | collective-permute-start | bytes 196616 | tf_op jit(solution)/shard_map/ppermute | solution.py:531
  334.2 8.4 %collective-permute-start.11 = (bf16[96,512]{1,0:T(8,128)(2,1)S(1)}, bf16[96,512]{1,0:T(8,128)(2,1)S(1)}, u32[]{:S(2)}, u32[]{:S(2)}) collective-permute-start(bf16[96,512]{1,0:T(8,128)(2,1)S(1)} %dynamic-slice_bitcast_fusion.13), channel_id=1, source_target_pairs={{0,16},{4,20},{8,24},{12,28},{16,0},{20,4},{24,8},{28,12},{1,17},{... | collective-permute-start | bytes 294920 | tf_op jit(solution)/shard_map/ppermute | solution.py:535
  339.2 7.6 %collective-permute-start.69 = (bf16[64,512]{1,0:T(8,128)(2,1)S(1)}, bf16[64,512]{1,0:T(8,128)(2,1)S(1)}, u32[]{:S(2)}, u32[]{:S(2)}) collective-permute-start(bf16[64,512]{1,0:T(8,128)(2,1)S(1)} %get-tuple-element.137), channel_id=1, source_target_pairs={{0,2},{1,3},{2,0},{3,1},{4,6},{5,7},{6,4},{7,5},{8,10},{9,11},{10,... | collective-permute-start | bytes 196616 | tf_op jit(solution)/shard_map/ppermute | solution.py:531
  347.9 6.7 %collective-permute-start.12 = (bf16[24,512]{1,0:T(8,128)(2,1)S(1)}, bf16[24,512]{1,0:T(8,128)(2,1)S(1)}, u32[]{:S(2)}, u32[]{:S(2)}) collective-permute-start(bf16[24,512]{1,0:T(8,128)(2,1)S(1)} %get-tuple-element.163), channel_id=1, source_target_pairs={{0,1},{1,2},{2,3},{3,0},{4,5},{5,6},{6,7},{7,4},{8,9},{9,10},{10,1... | collective-permute-start | bytes 73736 | tf_op jit(solution)/shard_map/ppermute | solution.py:531
  356.3 21.0 %collective-permute-start.71 = (bf16[256,512]{1,0:T(8,128)(2,1)S(1)}, bf16[256,512]{1,0:T(8,128)(2,1)S(1)}, u32[]{:S(2)}, u32[]{:S(2)}) collective-permute-start(bf16[256,512]{1,0:T(8,128)(2,1)S(1)} %bitcast.291), channel_id=1, source_target_pairs={{0,16},{4,20},{8,24},{12,28},{16,0},{20,4},{24,8},{28,12},{1,17},{... | collective-permute-start | bytes 786440 | tf_op jit(solution)/shard_map/ppermute | solution.py:535
  359.0 19.3 %collective-permute-start.59 = (bf16[256,512]{1,0:T(8,128)(2,1)S(1)}, bf16[256,512]{1,0:T(8,128)(2,1)S(1)}, u32[]{:S(2)}, u32[]{:S(2)}) collective-permute-start(bf16[256,512]{1,0:T(8,128)(2,1)S(1)} %bitcast.293), channel_id=1, source_target_pairs={{0,16},{4,20},{8,24},{12,28},{16,0},{20,4},{24,8},{28,12},{1,17},{... | collective-permute-start | bytes 786440 | tf_op jit(solution)/shard_map/ppermute | solution.py:535
  372.8 11.4 %collective-permute-start.36 = (bf16[384,512]{1,0:T(8,128)(2,1)S(1)}, bf16[384,512]{1,0:T(8,128)(2,1)S(1)}, u32[]{:S(2)}, u32[]{:S(2)}) collective-permute-start(bf16[384,512]{1,0:T(8,128)(2,1)S(1)} %maximum_select_fusion.11), channel_id=1, source_target_pairs={{0,8},{4,12},{8,0},{12,4},{16,24},{20,28},{24,16},{28,20},{1,9},{5... | collective-permute-start | bytes 1179656 | tf_op jit(solution)/shard_map/ppermute | solution.py:535
  375.9 10.4 %collective-permute-start.19 = (bf16[192,512]{1,0:T(8,128)(2,1)S(1)}, bf16[192,512]{1,0:T(8,128)(2,1)S(1)}, u32[]{:S(2)}, u32[]{:S(2)}) collective-permute-start(bf16[192,512]{1,0:T(8,128)(2,1)S(1)} %maximum_select_fusion.13), channel_id=1, source_target_pairs={{0,8},{4,12},{8,0},{12,4},{16,24},{20,28},{24,16},{28,20},{1,9},{5... | collective-permute-start | bytes 589832 | tf_op jit(solution)/shard_map/ppermute | solution.py:535
  377.6 20.5 %collective-permute-start.72 = (bf16[512,512]{1,0:T(8,128)(2,1)S(1)}, bf16[512,512]{1,0:T(8,128)(2,1)S(1)}, u32[]{:S(2)}, u32[]{:S(2)}) collective-permute-start(bf16[512,512]{1,0:T(8,128)(2,1)S(1)} %maximum_select_fusion.9), channel_id=1, source_target_pairs={{0,8},{4,12},{8,0},{12,4},{16,24},{20,28},{24,16},{28,20},{1,9},{5... | collective-permute-start | bytes 1572872 | tf_op jit(solution)/shard_map/ppermute | solution.py:535
  378.5 19.0 %collective-permute-start.60 = (bf16[512,512]{1,0:T(8,128)(2,1)S(1)}, bf16[512,512]{1,0:T(8,128)(2,1)S(1)}, u32[]{:S(2)}, u32[]{:S(2)}) collective-permute-start(bf16[512,512]{1,0:T(8,128)(2,1)S(1)} %maximum_select_fusion.8), channel_id=1, source_target_pairs={{0,8},{4,12},{8,0},{12,4},{16,24},{20,28},{24,16},{28,20},{1,9},{5... | collective-permute-start | bytes 1572872 | tf_op jit(solution)/shard_map/ppermute | solution.py:535
  384.5 17.8 %collective-permute-start.37 = (bf16[768,512]{1,0:T(8,128)(2,1)S(1)}, bf16[768,512]{1,0:T(8,128)(2,1)S(1)}, u32[]{:S(2)}, u32[]{:S(2)}) collective-permute-start(bf16[768,512]{1,0:T(8,128)(2,1)S(1)} %maximum_select_fusion.6), channel_id=1, source_target_pairs={{0,4},{4,0},{8,12},{12,8},{16,20},{20,16},{24,28},{28,24},{1,5},{5... | collective-permute-start | bytes 2359304 | tf_op jit(solution)/shard_map/ppermute | solution.py:535
  386.4 14.5 %collective-permute-start.20 = (bf16[384,512]{1,0:T(8,128)(2,1)S(1)}, bf16[384,512]{1,0:T(8,128)(2,1)S(1)}, u32[]{:S(2)}, u32[]{:S(2)}) collective-permute-start(bf16[384,512]{1,0:T(8,128)(2,1)S(1)} %maximum_select_fusion.10), channel_id=1, source_target_pairs={{0,4},{4,0},{8,12},{12,8},{16,20},{20,16},{24,28},{28,24},{1,5},{5... | collective-permute-start | bytes 1179656 | tf_op jit(solution)/shard_map/ppermute | solution.py:535
  398.0 10.0 %collective-permute-start.61 = (bf16[1024,512]{1,0:T(8,128)(2,1)S(1)}, bf16[1024,512]{1,0:T(8,128)(2,1)}, u32[]{:S(2)}, u32[]{:S(2)}) collective-permute-start(bf16[1024,512]{1,0:T(8,128)(2,1)S(1)} %maximum_select_fusion.3), channel_id=1, source_target_pairs={{0,4},{4,0},{8,12},{12,8},{16,20},{20,16},{24,28},{28,24},{1,5},{5... | collective-permute-start | bytes 3145736 | tf_op jit(solution)/shard_map/ppermute | solution.py:535
  398.6 18.9 %collective-permute-start.73 = (bf16[1024,512]{1,0:T(8,128)(2,1)S(1)}, bf16[1024,512]{1,0:T(8,128)(2,1)}, u32[]{:S(2)}, u32[]{:S(2)}) collective-permute-start(bf16[1024,512]{1,0:T(8,128)(2,1)S(1)} %maximum_select_fusion.4), channel_id=1, source_target_pairs={{0,4},{4,0},{8,12},{12,8},{16,20},{20,16},{24,28},{28,24},{1,5},{5... | collective-permute-start | bytes 3145736 | tf_op jit(solution)/shard_map/ppermute | solution.py:535
  (69 other events, 562.8 us)
